TPU v7x, 256 devices: a whole 4x4x8 slice. The times are simulated.
256 devices in a mesh: ctx: 8 (over x, core), grp: 32 (over y, z).
Axes of the slice: x: 4, y: 4, z: 8, core: 2. Of those that a mesh axis runs over, the one named last changes fastest.
Arguments:
- queries: bfloat16 [32, 1024, 8192], P('grp', 'ctx'), may hold values from -32 to 32
- keys: bfloat16 [32, 1024, 1024], P('grp', 'ctx'), may hold values from -32 to 32
- values: bfloat16 [32, 1024, 1024], P('grp', 'ctx'), may hold values from -6 to 6
- placement: int32 [32, 16], P('grp', 'ctx'), may hold values from 0 to 15, each once within a row
- lengths: int32 [32], replicated, may hold values from 1 to 32, 512 in all
Outputs:
- attended: bfloat16 [32, 1024, 8192], P('grp', 'ctx')
Inputs may be any that keep to these rules, and one draw needn't show every extreme that they name: `placement`: every row is a permutation of the stretches of its column. `lengths`: the entries sum to 512; some request takes exactly 32 stretches.
All inputs are finite; a program needn't handle non-finite values.
Results may differ from a plain program's by a relative error of at most 0.005.
Values may be sent and summed in bfloat16 or wider, within the bound.
A program may use at most 256 MiB of HBM per device.

v0:
```python
import math

import jax
import jax.numpy as jnp
from jax import lax
from jax.sharding import PartitionSpec as P

HD = 128
STRETCH = 64
SPAN = 3


NEG = -1e30


def from_behind(value, axis, steps):
    count = lax.axis_size(axis)
    first, last = (max(0, -steps), min(count, count - steps))
    return lax.ppermute(value, axis, [(source, source + steps) for source in range(first, last)])


def request_of(req_ends, stretch_ids):
    return jnp.sum((req_ends[None, :] <= stretch_ids[:, None]).astype(jnp.int32), axis=1)


def positions(slot_stretches, num_rows, column_idx, column_rows):
    within = jnp.arange(num_rows, dtype=jnp.int32)
    spread = jnp.repeat(slot_stretches, STRETCH, total_repeat_length=num_rows)
    return column_idx * column_rows + spread * STRETCH + within % STRETCH


def merge_block(running, local_q, key_rows, value_rows, visible):
    kv_heads = local_q.shape[1]
    keys_three = key_rows.reshape(key_rows.shape[0], kv_heads, HD)
    values_three = value_rows.reshape(value_rows.shape[0], kv_heads, HD)
    scores = jnp.einsum(
        "qhgd,khd->hgqk", local_q, keys_three, preferred_element_type=jnp.float32
    ) * (1.0 / math.sqrt(HD))
    masked = visible[None, None]
    run_max, run_sum, run_acc = running
    new_max = jnp.maximum(run_max, jnp.max(jnp.where(masked, scores, NEG), axis=-1))
    weights = jnp.where(masked, jnp.exp(scores - new_max[..., None]), 0.0)
    factor = jnp.exp(run_max - new_max)
    new_sum = run_sum * factor + jnp.sum(weights, axis=-1)
    partial_out = jnp.einsum(
        "hgqk,khd->qhgd",
        weights.astype(jnp.bfloat16),
        values_three,
        preferred_element_type=jnp.float32,
    )
    new_acc = run_acc * jnp.transpose(factor, (2, 0, 1))[..., None] + partial_out
    return (new_max, new_sum, new_acc)


def attend_block(running, local_q, key_rows, value_rows, visible):
    return merge_block(running, local_q, key_rows, value_rows, visible)


def body(queries, keys, values, placement, lengths):
    tok_rows = queries.shape[1]
    column_rows = tok_rows * lax.axis_size("ctx")
    kv_heads = keys.shape[2] // HD
    groups = queries.shape[2] // keys.shape[2]
    local_q = queries[0].reshape(tok_rows, kv_heads, groups, HD)
    local_k = keys[0]
    local_v = values[0]
    own_place = placement[0]
    req_ends = jnp.cumsum(lengths)
    column = lax.axis_index("grp")
    query_pos = positions(own_place, tok_rows, column, column_rows)
    query_req = request_of(req_ends, query_pos // STRETCH)
    running = (
        jnp.full((kv_heads, groups, tok_rows), NEG, jnp.float32),
        jnp.zeros((kv_heads, groups, tok_rows), jnp.float32),
        jnp.zeros((tok_rows, kv_heads, groups, HD), jnp.float32),
    )

    def attend_piece(state, key_rows, value_rows, key_place, column_idx):
        key_pos = positions(key_place, key_rows.shape[0], column_idx, column_rows)
        key_req = request_of(req_ends, key_pos // STRETCH)
        visible = (
            (column_idx >= 0)
            & (key_req[None, :] == query_req[:, None])
            & (key_pos[None, :] <= query_pos[:, None])
        )
        return attend_block(state, local_q, key_rows, value_rows, visible)

    def fold_column(state, whole_k, whole_v, whole_place, column_idx):
        key_block = 2 * tok_rows
        num_blocks = whole_k.shape[0] // key_block
        key_blocks = whole_k.reshape(num_blocks, key_block, whole_k.shape[1])
        value_blocks = whole_v.reshape(num_blocks, key_block, whole_v.shape[1])
        place_blocks = whole_place.reshape(num_blocks, key_block // STRETCH)

        def scan_step(inner, blocks_now):
            return (
                attend_piece(inner, blocks_now[0], blocks_now[1], blocks_now[2], column_idx),
                None,
            )

        result, _unused = lax.scan(scan_step, state, (key_blocks, value_blocks, place_blocks))
        return result

    whole_k, whole_v, whole_place = (
        lax.all_gather(local_k, "ctx", axis=0, tiled=True),
        lax.all_gather(local_v, "ctx", axis=0, tiled=True),
        lax.all_gather(own_place, "ctx", axis=0, tiled=True),
    )
    running = fold_column(running, whole_k, whole_v, whole_place, column)
    for shift_by in range(1, SPAN):
        moved_k, moved_v, moved_place = from_behind(
            (whole_k, whole_v, whole_place), "grp", shift_by
        )
        running = fold_column(running, moved_k, moved_v, moved_place, column - shift_by)
    run_max, run_sum, run_acc = running
    result = run_acc / jnp.transpose(run_sum, (2, 0, 1))[..., None]
    return result.astype(jnp.bfloat16).reshape(1, tok_rows, kv_heads * groups * HD)


def solution(mesh):
    in_specs = (
        P("grp", "ctx", None),
        P("grp", "ctx", None),
        P("grp", "ctx", None),
        P("grp", "ctx"),
        P(),
    )
    out_specs = P("grp", "ctx", None)
    return jax.shard_map(body, mesh=mesh, in_specs=in_specs, out_specs=out_specs, check_vma=False)
```

profile of v0, /device:TPU:88, one launch (start us, length us, event | category | flops | bytes accessed | tf_op | source)
XLA Modules:
  0.0 474.2 jit_solution(3657366843530942116)
XLA Ops:
  10.7 9.2 %all-reduce = s32[16]{0:T(128)S(1)} all-reduce(s32[16]{0:T(128)S(1)} %bitcast_dynamic-update-slice_fusion), channel_id=2, replica_groups=mesh['ctx'=8,'grp'=32] {'ctx'}, use_global_device_ids=true, to_apply=%add | all-reduce | flops 16 | bytes 128 | tf_op jit(solution)/shard_map/all_gather | solution.py:107
  19.9 3.8 collective-permute-start
  23.7 5.5 %collective-permute-start.3 = (s32[16]{0:T(128)S(1)}, s32[16]{0:T(128)S(1)}, u32[]{:S(2)}, u32[]{:S(2)}) collective-permute-start(s32[16]{0:T(128)S(1)} %all-reduce), channel_id=1, source_target_pairs={{0,2},{1,3},{2,4},{3,5},{4,6},{5,7},{6,8},{7,9},{8,10},{9,11},{10,... | collective-permute-start | bytes 200 | tf_op jit(solution)/shard_map/ppermute | solution.py:19
  30.2 4.1 copy.51
  36.2 3.0 copy.53
  39.4 3.0 collective-permute-start.1
  42.5 4.7 collective-permute-start.4
  47.1 21.7 %all-gather.8.cloned.1.call-done = bf16[1,1024,1024]{2,1,0:T(8,128)(2,1)} async-done(((bf16[1,128,1024]{2,1,0:T(8,128)(2,1)}), bf16[1,1024,1024]{2,1,0:T(8,128)(2,1)}) %all-gather.8.cloned.1.call-update) | async-done | bytes 2097168 | tf_op jit(solution)/shard_map/all_gather | solution.py:106
  68.8 3.5 collective-permute-start.2
  72.3 4.8 %collective-permute-start.5 = (bf16[1024,1024]{1,0:T(8,128)(2,1)}, bf16[1024,1024]{1,0:T(8,128)(2,1)}, u32[]{:S(2)}, u32[]{:S(2)}) collective-permute-start(bf16[1024,1024]{1,0:T(8,128)(2,1)} %bitcast.246), channel_id=1, source_target_pairs={{0,2},{1,3},{2,4},{3,5},{4,6},{5,7},{6,8},{7,9},{8,10},{9,11},{10,... | collective-permute-start | bytes 6291464 | tf_op jit(solution)/shard_map/ppermute | solution.py:19
  77.1 95.0 %while.65 = (s32[]{:T(128)}, f32[8,8,128]{2,1,0:T(8,128)S(1)}, f32[8,8,128]{2,1,0:T(8,128)S(1)}, f32[128,8,8,128]{0,3,2,1:T(8,128)}, pred[]{:T(512)}, /*index=5*...) while((s32[]{:T(128)}, f32[8,8,128]{2,1,0:T(8,128)S(1)}, ...), condition=%wide.region_6.8_spmd.clone.clone.clone, body=%wide.region_2.7_spmd.clone.clone.clone.sunk | while | flops 1100172032 | bytes 75113544 | solution.py:101
  77.8 2.6 and_select_fusion.19
  84.1 5.7 %fusion.146 = (f32[8,8,128]{2,1,0:T(8,128)S(1)}, f32[8,256,128,8]{2,1,3,0:T(8,128)}) fusion(pred[128,256]{0,1:T(8,128)(4,1)S(1)} %compare_and_fusion.8, bf16[256,8,128,1]{0,2,3,1:T(8,128)(2,1)} %bitcast.236, bf16[128,8,8,128]{3,0,2,1:T(8,128)(2,1)S(1)} %get-tuple-element.1796), kind=kOutput, calls=%fused_computation.85.clone.1 | convolution fusion | flops 543154176 | bytes 11075584 | tf_op jit(solution)/shard_map/while/body/eval_jaxpr/qhgd,khd->hgqk/dot_general | solution.py:36
  90.0 7.5 %bitcast_add_fusion.8 = f32[128,8,8,128]{0,3,2,1:T(8,128)} fusion(f32[128,8,8,128]{0,3,2,1:T(8,128)} %get-tuple-element.1771, f32[128,8,8]{0,2,1:T(8,128)S(1)} %get-tuple-element.1748, pred[]{:T(512)S(6)} %compare.165, bf16[256,8,128,1]{0,2,3,1:T(8,128)(2,1)S(1)} %bitcast.233, f32[8,256,128,8]{2,1,3,0:T(8,128)} %get-tuple-element.1747, ...), kind=kOutput, calls=%fused_computation.91.clone.1 | convolution fusion | flops 548405248 | bytes 17399808 | tf_op jit(solution)/shard_map/while/body/eval_jaxpr/hgqk,khd->qhgd/dot_general | solution.py:45
  97.6 2.3 fusion.148
  100.6 2.6 and_select_fusion.19
  107.0 5.7 %fusion.146 = (f32[8,8,128]{2,1,0:T(8,128)S(1)}, f32[8,256,128,8]{2,1,3,0:T(8,128)}) fusion(pred[128,256]{0,1:T(8,128)(4,1)S(1)} %compare_and_fusion.8, bf16[256,8,128,1]{0,2,3,1:T(8,128)(2,1)} %bitcast.236, bf16[128,8,8,128]{3,0,2,1:T(8,128)(2,1)S(1)} %get-tuple-element.1796), kind=kOutput, calls=%fused_computation.85.clone.1 | convolution fusion | flops 543154176 | bytes 11075584 | tf_op jit(solution)/shard_map/while/body/eval_jaxpr/qhgd,khd->hgqk/dot_general | solution.py:36
  112.9 8.7 %bitcast_add_fusion.8 = f32[128,8,8,128]{0,3,2,1:T(8,128)} fusion(f32[128,8,8,128]{0,3,2,1:T(8,128)} %get-tuple-element.1771, f32[128,8,8]{0,2,1:T(8,128)S(1)} %get-tuple-element.1748, pred[]{:T(512)S(6)} %compare.165, bf16[256,8,128,1]{0,2,3,1:T(8,128)(2,1)S(1)} %bitcast.233, f32[8,256,128,8]{2,1,3,0:T(8,128)} %get-tuple-element.1747, ...), kind=kOutput, calls=%fused_computation.91.clone.1 | convolution fusion | flops 548405248 | bytes 17399808 | tf_op jit(solution)/shard_map/while/body/eval_jaxpr/hgqk,khd->qhgd/dot_general | solution.py:45
  121.6 2.3 fusion.148
  124.7 2.6 and_select_fusion.19
  131.0 5.7 %fusion.146 = (f32[8,8,128]{2,1,0:T(8,128)S(1)}, f32[8,256,128,8]{2,1,3,0:T(8,128)}) fusion(pred[128,256]{0,1:T(8,128)(4,1)S(1)} %compare_and_fusion.8, bf16[256,8,128,1]{0,2,3,1:T(8,128)(2,1)} %bitcast.236, bf16[128,8,8,128]{3,0,2,1:T(8,128)(2,1)S(1)} %get-tuple-element.1796), kind=kOutput, calls=%fused_computation.85.clone.1 | convolution fusion | flops 543154176 | bytes 11075584 | tf_op jit(solution)/shard_map/while/body/eval_jaxpr/qhgd,khd->hgqk/dot_general | solution.py:36
  136.9 8.7 %bitcast_add_fusion.8 = f32[128,8,8,128]{0,3,2,1:T(8,128)} fusion(f32[128,8,8,128]{0,3,2,1:T(8,128)} %get-tuple-element.1771, f32[128,8,8]{0,2,1:T(8,128)S(1)} %get-tuple-element.1748, pred[]{:T(512)S(6)} %compare.165, bf16[256,8,128,1]{0,2,3,1:T(8,128)(2,1)S(1)} %bitcast.233, f32[8,256,128,8]{2,1,3,0:T(8,128)} %get-tuple-element.1747, ...), kind=kOutput, calls=%fused_computation.91.clone.1 | convolution fusion | flops 548405248 | bytes 17399808 | tf_op jit(solution)/shard_map/while/body/eval_jaxpr/hgqk,khd->qhgd/dot_general | solution.py:45
  145.7 2.3 fusion.148
  148.7 2.6 and_select_fusion.19
  155.1 5.7 %fusion.146 = (f32[8,8,128]{2,1,0:T(8,128)S(1)}, f32[8,256,128,8]{2,1,3,0:T(8,128)}) fusion(pred[128,256]{0,1:T(8,128)(4,1)S(1)} %compare_and_fusion.8, bf16[256,8,128,1]{0,2,3,1:T(8,128)(2,1)} %bitcast.236, bf16[128,8,8,128]{3,0,2,1:T(8,128)(2,1)S(1)} %get-tuple-element.1796), kind=kOutput, calls=%fused_computation.85.clone.1 | convolution fusion | flops 543154176 | bytes 11075584 | tf_op jit(solution)/shard_map/while/body/eval_jaxpr/qhgd,khd->hgqk/dot_general | solution.py:36
  161.0 8.7 %bitcast_add_fusion.8 = f32[128,8,8,128]{0,3,2,1:T(8,128)} fusion(f32[128,8,8,128]{0,3,2,1:T(8,128)} %get-tuple-element.1771, f32[128,8,8]{0,2,1:T(8,128)S(1)} %get-tuple-element.1748, pred[]{:T(512)S(6)} %compare.165, bf16[256,8,128,1]{0,2,3,1:T(8,128)(2,1)S(1)} %bitcast.233, f32[8,256,128,8]{2,1,3,0:T(8,128)} %get-tuple-element.1747, ...), kind=kOutput, calls=%fused_computation.91.clone.1 | convolution fusion | flops 548405248 | bytes 17399808 | tf_op jit(solution)/shard_map/while/body/eval_jaxpr/hgqk,khd->qhgd/dot_general | solution.py:45
  169.7 2.3 fusion.148
  172.1 97.9 %collective-permute-done.2 = bf16[1024,1024]{1,0:T(8,128)(2,1)} collective-permute-done((bf16[1024,1024]{1,0:T(8,128)(2,1)}, bf16[1024,1024]{1,0:T(8,128)(2,1)}, u32[]{:S(2)}, u32[]{:S(2)}) %collective-permute-start.2) | collective-permute-done | bytes 2097184 | tf_op jit(solution)/shard_map/ppermute | solution.py:19
  270.0 95.7 %while.63 = (s32[]{:T(128)}, f32[8,8,128]{2,1,0:T(8,128)S(1)}, f32[8,8,128]{2,1,0:T(8,128)S(1)}, f32[128,8,8,128]{0,3,2,1:T(8,128)}, pred[]{:T(512)}, /*index=5*...) while((s32[]{:T(128)}, f32[8,8,128]{2,1,0:T(8,128)S(1)}, ...), condition=%wide.region_11.13_spmd.clone, body=%wide.region_7.12_spmd.clone.sunk | while | flops 1099098880 | bytes 75113528 | solution.py:101
  270.7 2.6 and_select_fusion.17
  277.0 5.7 %fusion.126 = (f32[8,8,128]{2,1,0:T(8,128)S(1)}, f32[8,256,128,8]{2,1,3,0:T(8,128)}) fusion(pred[128,256]{0,1:T(8,128)(4,1)S(1)} %compare_and_fusion.6, bf16[256,8,128,1]{0,2,3,1:T(8,128)(2,1)} %bitcast.237, bf16[128,8,8,128]{3,0,2,1:T(8,128)(2,1)S(1)} %get-tuple-element.1850), kind=kOutput, calls=%fused_computation.5.clone.1 | convolution fusion | flops 543154176 | bytes 11075584 | tf_op jit(solution)/shard_map/while/body/eval_jaxpr/qhgd,khd->hgqk/dot_general | solution.py:36
  283.0 8.6 %bitcast_add_fusion.6 = f32[128,8,8,128]{0,3,2,1:T(8,128)} fusion(f32[128,8,8,128]{0,3,2,1:T(8,128)} %get-tuple-element.1825, f32[128,8,8]{0,2,1:T(8,128)S(1)} %get-tuple-element.1695, bf16[256,8,128,1]{0,2,3,1:T(8,128)(2,1)S(1)} %bitcast.234, f32[8,256,128,8]{2,1,3,0:T(8,128)} %get-tuple-element.1694, f32[8,8,128]{2,1,0:T(8,128)S(1)} %get-tuple-element.1841, ...), kind=kOutput, calls=%fused_computation.11.clone.1 | convolution fusion | flops 547356672 | bytes 17399808 | tf_op jit(solution)/shard_map/while/body/eval_jaxpr/hgqk,khd->qhgd/dot_general | solution.py:45
  291.6 2.3 fusion.128
  294.6 2.6 and_select_fusion.17
  301.0 5.7 %fusion.126 = (f32[8,8,128]{2,1,0:T(8,128)S(1)}, f32[8,256,128,8]{2,1,3,0:T(8,128)}) fusion(pred[128,256]{0,1:T(8,128)(4,1)S(1)} %compare_and_fusion.6, bf16[256,8,128,1]{0,2,3,1:T(8,128)(2,1)} %bitcast.237, bf16[128,8,8,128]{3,0,2,1:T(8,128)(2,1)S(1)} %get-tuple-element.1850), kind=kOutput, calls=%fused_computation.5.clone.1 | convolution fusion | flops 543154176 | bytes 11075584 | tf_op jit(solution)/shard_map/while/body/eval_jaxpr/qhgd,khd->hgqk/dot_general | solution.py:36
  306.9 8.6 %bitcast_add_fusion.6 = f32[128,8,8,128]{0,3,2,1:T(8,128)} fusion(f32[128,8,8,128]{0,3,2,1:T(8,128)} %get-tuple-element.1825, f32[128,8,8]{0,2,1:T(8,128)S(1)} %get-tuple-element.1695, bf16[256,8,128,1]{0,2,3,1:T(8,128)(2,1)S(1)} %bitcast.234, f32[8,256,128,8]{2,1,3,0:T(8,128)} %get-tuple-element.1694, f32[8,8,128]{2,1,0:T(8,128)S(1)} %get-tuple-element.1841, ...), kind=kOutput, calls=%fused_computation.11.clone.1 | convolution fusion | flops 547356672 | bytes 17399808 | tf_op jit(solution)/shard_map/while/body/eval_jaxpr/hgqk,khd->qhgd/dot_general | solution.py:45
  315.5 2.3 fusion.128
  318.6 2.6 and_select_fusion.17
  324.9 5.7 %fusion.126 = (f32[8,8,128]{2,1,0:T(8,128)S(1)}, f32[8,256,128,8]{2,1,3,0:T(8,128)}) fusion(pred[128,256]{0,1:T(8,128)(4,1)S(1)} %compare_and_fusion.6, bf16[256,8,128,1]{0,2,3,1:T(8,128)(2,1)} %bitcast.237, bf16[128,8,8,128]{3,0,2,1:T(8,128)(2,1)S(1)} %get-tuple-element.1850), kind=kOutput, calls=%fused_computation.5.clone.1 | convolution fusion | flops 543154176 | bytes 11075584 | tf_op jit(solution)/shard_map/while/body/eval_jaxpr/qhgd,khd->hgqk/dot_general | solution.py:36
  330.8 8.6 %bitcast_add_fusion.6 = f32[128,8,8,128]{0,3,2,1:T(8,128)} fusion(f32[128,8,8,128]{0,3,2,1:T(8,128)} %get-tuple-element.1825, f32[128,8,8]{0,2,1:T(8,128)S(1)} %get-tuple-element.1695, bf16[256,8,128,1]{0,2,3,1:T(8,128)(2,1)S(1)} %bitcast.234, f32[8,256,128,8]{2,1,3,0:T(8,128)} %get-tuple-element.1694, f32[8,8,128]{2,1,0:T(8,128)S(1)} %get-tuple-element.1841, ...), kind=kOutput, calls=%fused_computation.11.clone.1 | convolution fusion | flops 547356672 | bytes 17399808 | tf_op jit(solution)/shard_map/while/body/eval_jaxpr/hgqk,khd->qhgd/dot_general | solution.py:45
  339.5 2.3 fusion.128
  342.5 2.6 and_select_fusion.17
  348.8 5.7 %fusion.126 = (f32[8,8,128]{2,1,0:T(8,128)S(1)}, f32[8,256,128,8]{2,1,3,0:T(8,128)}) fusion(pred[128,256]{0,1:T(8,128)(4,1)S(1)} %compare_and_fusion.6, bf16[256,8,128,1]{0,2,3,1:T(8,128)(2,1)} %bitcast.237, bf16[128,8,8,128]{3,0,2,1:T(8,128)(2,1)S(1)} %get-tuple-element.1850), kind=kOutput, calls=%fused_computation.5.clone.1 | convolution fusion | flops 543154176 | bytes 11075584 | tf_op jit(solution)/shard_map/while/body/eval_jaxpr/qhgd,khd->hgqk/dot_general | solution.py:36
  354.8 8.6 %bitcast_add_fusion.6 = f32[128,8,8,128]{0,3,2,1:T(8,128)} fusion(f32[128,8,8,128]{0,3,2,1:T(8,128)} %get-tuple-element.1825, f32[128,8,8]{0,2,1:T(8,128)S(1)} %get-tuple-element.1695, bf16[256,8,128,1]{0,2,3,1:T(8,128)(2,1)S(1)} %bitcast.234, f32[8,256,128,8]{2,1,3,0:T(8,128)} %get-tuple-element.1694, f32[8,8,128]{2,1,0:T(8,128)S(1)} %get-tuple-element.1841, ...), kind=kOutput, calls=%fused_computation.11.clone.1 | convolution fusion | flops 547356672 | bytes 17399808 | tf_op jit(solution)/shard_map/while/body/eval_jaxpr/hgqk,khd->qhgd/dot_general | solution.py:45
  363.4 2.3 fusion.128
  365.8 96.0 %while.64 = (s32[]{:T(128)}, f32[8,8,128]{2,1,0:T(8,128)S(1)}, f32[8,8,128]{2,1,0:T(8,128)S(1)}, f32[128,8,8,128]{0,3,2,1:T(8,128)}, pred[]{:T(512)}, /*index=5*...) while((s32[]{:T(128)}, f32[8,8,128]{2,1,0:T(8,128)S(1)}, ...), condition=%wide.region_16.18_spmd.clone, body=%wide.region_12.17_spmd.clone.sunk | while | flops 1099098880 | bytes 75113528 | solution.py:101
  366.7 2.6 and_select_fusion.18
  373.0 5.7 %fusion.136 = (f32[8,8,128]{2,1,0:T(8,128)S(1)}, f32[8,256,128,8]{2,1,3,0:T(8,128)}) fusion(pred[128,256]{0,1:T(8,128)(4,1)S(1)} %compare_and_fusion.7, bf16[256,8,128,1]{0,2,3,1:T(8,128)(2,1)} %bitcast.238, bf16[128,8,8,128]{3,0,2,1:T(8,128)(2,1)S(1)} %get-tuple-element.1904), kind=kOutput, calls=%fused_computation.45.clone.1 | convolution fusion | flops 543154176 | bytes 11075584 | tf_op jit(solution)/shard_map/while/body/eval_jaxpr/qhgd,khd->hgqk/dot_general | solution.py:36
  379.0 8.6 %bitcast_add_fusion.7 = f32[128,8,8,128]{0,3,2,1:T(8,128)} fusion(f32[128,8,8,128]{0,3,2,1:T(8,128)} %get-tuple-element.1879, f32[128,8,8]{0,2,1:T(8,128)S(1)} %get-tuple-element.1722, bf16[256,8,128,1]{0,2,3,1:T(8,128)(2,1)S(1)} %bitcast.235, f32[8,256,128,8]{2,1,3,0:T(8,128)} %get-tuple-element.1721, f32[8,8,128]{2,1,0:T(8,128)S(1)} %get-tuple-element.1895, ...), kind=kOutput, calls=%fused_computation.51.clone.1 | convolution fusion | flops 547356672 | bytes 17399808 | tf_op jit(solution)/shard_map/while/body/eval_jaxpr/hgqk,khd->qhgd/dot_general | solution.py:45
  387.6 2.3 fusion.138
  390.6 2.6 and_select_fusion.18
  397.0 5.7 %fusion.136 = (f32[8,8,128]{2,1,0:T(8,128)S(1)}, f32[8,256,128,8]{2,1,3,0:T(8,128)}) fusion(pred[128,256]{0,1:T(8,128)(4,1)S(1)} %compare_and_fusion.7, bf16[256,8,128,1]{0,2,3,1:T(8,128)(2,1)} %bitcast.238, bf16[128,8,8,128]{3,0,2,1:T(8,128)(2,1)S(1)} %get-tuple-element.1904), kind=kOutput, calls=%fused_computation.45.clone.1 | convolution fusion | flops 543154176 | bytes 11075584 | tf_op jit(solution)/shard_map/while/body/eval_jaxpr/qhgd,khd->hgqk/dot_general | solution.py:36
  402.9 8.6 %bitcast_add_fusion.7 = f32[128,8,8,128]{0,3,2,1:T(8,128)} fusion(f32[128,8,8,128]{0,3,2,1:T(8,128)} %get-tuple-element.1879, f32[128,8,8]{0,2,1:T(8,128)S(1)} %get-tuple-element.1722, bf16[256,8,128,1]{0,2,3,1:T(8,128)(2,1)S(1)} %bitcast.235, f32[8,256,128,8]{2,1,3,0:T(8,128)} %get-tuple-element.1721, f32[8,8,128]{2,1,0:T(8,128)S(1)} %get-tuple-element.1895, ...), kind=kOutput, calls=%fused_computation.51.clone.1 | convolution fusion | flops 547356672 | bytes 17399808 | tf_op jit(solution)/shard_map/while/body/eval_jaxpr/hgqk,khd->qhgd/dot_general | solution.py:45
  411.5 2.3 fusion.138
  414.5 2.6 and_select_fusion.18
  420.9 5.7 %fusion.136 = (f32[8,8,128]{2,1,0:T(8,128)S(1)}, f32[8,256,128,8]{2,1,3,0:T(8,128)}) fusion(pred[128,256]{0,1:T(8,128)(4,1)S(1)} %compare_and_fusion.7, bf16[256,8,128,1]{0,2,3,1:T(8,128)(2,1)} %bitcast.238, bf16[128,8,8,128]{3,0,2,1:T(8,128)(2,1)S(1)} %get-tuple-element.1904), kind=kOutput, calls=%fused_computation.45.clone.1 | convolution fusion | flops 543154176 | bytes 11075584 | tf_op jit(solution)/shard_map/while/body/eval_jaxpr/qhgd,khd->hgqk/dot_general | solution.py:36
  426.8 8.6 %bitcast_add_fusion.7 = f32[128,8,8,128]{0,3,2,1:T(8,128)} fusion(f32[128,8,8,128]{0,3,2,1:T(8,128)} %get-tuple-element.1879, f32[128,8,8]{0,2,1:T(8,128)S(1)} %get-tuple-element.1722, bf16[256,8,128,1]{0,2,3,1:T(8,128)(2,1)S(1)} %bitcast.235, f32[8,256,128,8]{2,1,3,0:T(8,128)} %get-tuple-element.1721, f32[8,8,128]{2,1,0:T(8,128)S(1)} %get-tuple-element.1895, ...), kind=kOutput, calls=%fused_computation.51.clone.1 | convolution fusion | flops 547356672 | bytes 17399808 | tf_op jit(solution)/shard_map/while/body/eval_jaxpr/hgqk,khd->qhgd/dot_general | solution.py:45
  435.4 2.3 fusion.138
  438.5 2.6 and_select_fusion.18
  444.8 5.7 %fusion.136 = (f32[8,8,128]{2,1,0:T(8,128)S(1)}, f32[8,256,128,8]{2,1,3,0:T(8,128)}) fusion(pred[128,256]{0,1:T(8,128)(4,1)S(1)} %compare_and_fusion.7, bf16[256,8,128,1]{0,2,3,1:T(8,128)(2,1)} %bitcast.238, bf16[128,8,8,128]{3,0,2,1:T(8,128)(2,1)S(1)} %get-tuple-element.1904), kind=kOutput, calls=%fused_computation.45.clone.1 | convolution fusion | flops 543154176 | bytes 11075584 | tf_op jit(solution)/shard_map/while/body/eval_jaxpr/qhgd,khd->hgqk/dot_general | solution.py:36
  450.8 8.6 %bitcast_add_fusion.7 = f32[128,8,8,128]{0,3,2,1:T(8,128)} fusion(f32[128,8,8,128]{0,3,2,1:T(8,128)} %get-tuple-element.1879, f32[128,8,8]{0,2,1:T(8,128)S(1)} %get-tuple-element.1722, bf16[256,8,128,1]{0,2,3,1:T(8,128)(2,1)S(1)} %bitcast.235, f32[8,256,128,8]{2,1,3,0:T(8,128)} %get-tuple-element.1721, f32[8,8,128]{2,1,0:T(8,128)S(1)} %get-tuple-element.1895, ...), kind=kOutput, calls=%fused_computation.51.clone.1 | convolution fusion | flops 547356672 | bytes 17399808 | tf_op jit(solution)/shard_map/while/body/eval_jaxpr/hgqk,khd->qhgd/dot_general | solution.py:45
  459.4 2.3 fusion.138
  461.7 2.8 divide_convert_fusion
  464.5 2.9 copy.71
  (199 shorter events, 62.0 us)
Async XLA Ops:
  6.5 28.4 %copy-start.4 = (pred[128]{0:T(512)(128)(4,1)S(1)}, pred[128]{0:T(512)(128)(4,1)}, u32[]{:S(2)}) copy-start(pred[128]{0:T(512)(128)(4,1)} %constant.739) | copy-start | bytes 388
  6.5 27.8 %copy-start.5 = (s32[1,2]{1,0:T(1,128)S(1)}, s32[1,2]{1,0:T(1,128)}, u32[]{:S(2)}) copy-start(s32[1,2]{1,0:T(1,128)} %param.24) | copy-start | bytes 28
  6.5 32.9 %all-gather.6.cloned.1.call-start = ((), (), s32[]{:S(2)}) async-start(), calls=%async_computation | async-start | bytes 2359296 | tf_op jit(solution)/shard_map/all_gather | solution.py:105
  7.3 61.6 %all-gather.8.cloned.1.call-start = ((), (), s32[]{:S(2)}) async-start(), calls=%async_computation.1 | async-start | bytes 2359296 | tf_op jit(solution)/shard_map/all_gather | solution.py:106
  19.9 19.3 %collective-permute-start = (s32[16]{0:T(128)S(1)}, s32[16]{0:T(128)S(1)}, u32[]{:S(2)}, u32[]{:S(2)}) collective-permute-start(s32[16]{0:T(128)S(1)} %all-reduce), channel_id=1, source_target_pairs={{0,1},{1,2},{2,3},{3,4},{4,5},{5,6},{6,7},{7,8},{8,9},{9,10},{10,1... | collective-permute-start | bytes 200 | tf_op jit(solution)/shard_map/ppermute | solution.py:19
  23.7 15.6 %collective-permute-start.3 = (s32[16]{0:T(128)S(1)}, s32[16]{0:T(128)S(1)}, u32[]{:S(2)}, u32[]{:S(2)}) collective-permute-start(s32[16]{0:T(128)S(1)} %all-reduce), channel_id=1, source_target_pairs={{0,2},{1,3},{2,4},{3,5},{4,6},{5,7},{6,8},{7,9},{8,10},{9,11},{10,... | collective-permute-start | bytes 200 | tf_op jit(solution)/shard_map/ppermute | solution.py:19
  30.2 46.8 %copy-start.3 = (s32[2,128]{1,0:T(2,128)S(1)}, s32[2,128]{1,0:T(2,128)}, u32[]{:S(2)}) copy-start(s32[2,128]{1,0:T(2,128)} %constant.685.clone.2) | copy-start | bytes 3076
  39.4 230.6 %collective-permute-start.1 = (bf16[1024,1024]{1,0:T(8,128)(2,1)}, bf16[1024,1024]{1,0:T(8,128)(2,1)}, u32[]{:S(2)}, u32[]{:S(2)}) collective-permute-start(bf16[1024,1024]{1,0:T(8,128)(2,1)} %bitcast.242), channel_id=1, source_target_pairs={{0,1},{1,2},{2,3},{3,4},{4,5},{5,6},{6,7},{7,8},{8,9},{9,10},{10,1... | collective-permute-start | bytes 6291464 | tf_op jit(solution)/shard_map/ppermute | solution.py:19
  42.5 323.3 %collective-permute-start.4 = (bf16[1024,1024]{1,0:T(8,128)(2,1)}, bf16[1024,1024]{1,0:T(8,128)(2,1)}, u32[]{:S(2)}, u32[]{:S(2)}) collective-permute-start(bf16[1024,1024]{1,0:T(8,128)(2,1)} %bitcast.243), channel_id=1, source_target_pairs={{0,2},{1,3},{2,4},{3,5},{4,6},{5,7},{6,8},{7,9},{8,10},{9,11},{10,... | collective-permute-start | bytes 6291464 | tf_op jit(solution)/shard_map/ppermute | solution.py:19
  68.8 201.2 %collective-permute-start.2 = (bf16[1024,1024]{1,0:T(8,128)(2,1)}, bf16[1024,1024]{1,0:T(8,128)(2,1)}, u32[]{:S(2)}, u32[]{:S(2)}) collective-permute-start(bf16[1024,1024]{1,0:T(8,128)(2,1)} %bitcast.245), channel_id=1, source_target_pairs={{0,1},{1,2},{2,3},{3,4},{4,5},{5,6},{6,7},{7,8},{8,9},{9,10},{10,1... | collective-permute-start | bytes 6291464 | tf_op jit(solution)/shard_map/ppermute | solution.py:19
  72.3 293.5 %collective-permute-start.5 = (bf16[1024,1024]{1,0:T(8,128)(2,1)}, bf16[1024,1024]{1,0:T(8,128)(2,1)}, u32[]{:S(2)}, u32[]{:S(2)}) collective-permute-start(bf16[1024,1024]{1,0:T(8,128)(2,1)} %bitcast.246), channel_id=1, source_target_pairs={{0,2},{1,3},{2,4},{3,5},{4,6},{5,7},{6,8},{7,9},{8,10},{9,11},{10,... | collective-permute-start | bytes 6291464 | tf_op jit(solution)/shard_map/ppermute | solution.py:19
  90.0 7.6 %copy-start = (f32[8,256,128,8]{2,1,3,0:T(8,128)S(1)}, f32[8,256,128,8]{2,1,3,0:T(8,128)}, u32[]{:S(2)}) copy-start(f32[8,256,128,8]{2,1,3,0:T(8,128)} %get-tuple-element.1747) | copy-start | bytes 25165828 | tf_op jit(solution)/shard_map/while
  112.9 8.8 %copy-start = (f32[8,256,128,8]{2,1,3,0:T(8,128)S(1)}, f32[8,256,128,8]{2,1,3,0:T(8,128)}, u32[]{:S(2)}) copy-start(f32[8,256,128,8]{2,1,3,0:T(8,128)} %get-tuple-element.1747) | copy-start | bytes 25165828 | tf_op jit(solution)/shard_map/while
  136.9 8.8 %copy-start = (f32[8,256,128,8]{2,1,3,0:T(8,128)S(1)}, f32[8,256,128,8]{2,1,3,0:T(8,128)}, u32[]{:S(2)}) copy-start(f32[8,256,128,8]{2,1,3,0:T(8,128)} %get-tuple-element.1747) | copy-start | bytes 25165828 | tf_op jit(solution)/shard_map/while
  161.0 8.8 %copy-start = (f32[8,256,128,8]{2,1,3,0:T(8,128)S(1)}, f32[8,256,128,8]{2,1,3,0:T(8,128)}, u32[]{:S(2)}) copy-start(f32[8,256,128,8]{2,1,3,0:T(8,128)} %get-tuple-element.1747) | copy-start | bytes 25165828 | tf_op jit(solution)/shard_map/while
  283.0 8.6 %copy-start.1 = (f32[8,256,128,8]{2,1,3,0:T(8,128)S(1)}, f32[8,256,128,8]{2,1,3,0:T(8,128)}, u32[]{:S(2)}) copy-start(f32[8,256,128,8]{2,1,3,0:T(8,128)} %get-tuple-element.1694) | copy-start | bytes 25165828 | tf_op jit(solution)/shard_map/while
  306.9 8.6 %copy-start.1 = (f32[8,256,128,8]{2,1,3,0:T(8,128)S(1)}, f32[8,256,128,8]{2,1,3,0:T(8,128)}, u32[]{:S(2)}) copy-start(f32[8,256,128,8]{2,1,3,0:T(8,128)} %get-tuple-element.1694) | copy-start | bytes 25165828 | tf_op jit(solution)/shard_map/while
  330.8 8.6 %copy-start.1 = (f32[8,256,128,8]{2,1,3,0:T(8,128)S(1)}, f32[8,256,128,8]{2,1,3,0:T(8,128)}, u32[]{:S(2)}) copy-start(f32[8,256,128,8]{2,1,3,0:T(8,128)} %get-tuple-element.1694) | copy-start | bytes 25165828 | tf_op jit(solution)/shard_map/while
  354.8 8.6 %copy-start.1 = (f32[8,256,128,8]{2,1,3,0:T(8,128)S(1)}, f32[8,256,128,8]{2,1,3,0:T(8,128)}, u32[]{:S(2)}) copy-start(f32[8,256,128,8]{2,1,3,0:T(8,128)} %get-tuple-element.1694) | copy-start | bytes 25165828 | tf_op jit(solution)/shard_map/while
  378.9 8.6 %copy-start.2 = (f32[8,256,128,8]{2,1,3,0:T(8,128)S(1)}, f32[8,256,128,8]{2,1,3,0:T(8,128)}, u32[]{:S(2)}) copy-start(f32[8,256,128,8]{2,1,3,0:T(8,128)} %get-tuple-element.1721) | copy-start | bytes 25165828 | tf_op jit(solution)/shard_map/while
  402.9 8.6 %copy-start.2 = (f32[8,256,128,8]{2,1,3,0:T(8,128)S(1)}, f32[8,256,128,8]{2,1,3,0:T(8,128)}, u32[]{:S(2)}) copy-start(f32[8,256,128,8]{2,1,3,0:T(8,128)} %get-tuple-element.1721) | copy-start | bytes 25165828 | tf_op jit(solution)/shard_map/while
  426.8 8.6 %copy-start.2 = (f32[8,256,128,8]{2,1,3,0:T(8,128)S(1)}, f32[8,256,128,8]{2,1,3,0:T(8,128)}, u32[]{:S(2)}) copy-start(f32[8,256,128,8]{2,1,3,0:T(8,128)} %get-tuple-element.1721) | copy-start | bytes 25165828 | tf_op jit(solution)/shard_map/while
  450.7 8.6 %copy-start.2 = (f32[8,256,128,8]{2,1,3,0:T(8,128)S(1)}, f32[8,256,128,8]{2,1,3,0:T(8,128)}, u32[]{:S(2)}) copy-start(f32[8,256,128,8]{2,1,3,0:T(8,128)} %get-tuple-element.1721) | copy-start | bytes 25165828 | tf_op jit(solution)/shard_map/while
Sparse Core Ops, SparseCore 0:
  9.2 29.6 all-gather.5
  40.8 28.0 all-gather.7
where the time goes:
time: 476 us; the launch traced here: 474 us
  matrix products  171 us (36%)
  waiting for transfers between devices  121 us (25%)
  other arithmetic  80.7 us (17%)
  local copies, waits for them, and re-layouts  51.5 us (11%)
  starting transfers between devices  25.2 us (5%)
  between operations  14.2 us (3%)
  blocking collectives  9.22 us (2%)
    dot_general x12, matrix products, merge_block(): jnp.einsum('hgqk,khd->qhgd', weights.astype(jnp.bfloat16), values_three,...  103 us
    ppermute x6, waiting for transfers between devices, from_behind(): lax.ppermute(value, axis, [(source, source + steps) for source in range(f...  97.9 us
    dot_general x12, matrix products, merge_block(): jnp.einsum('qhgd,khd->hgqk', local_q, keys_three, preferred_element_type=...  68.4 us
    select_n x12, other arithmetic, attend_piece(): key_req = request_of(req_ends, key_pos // STRETCH)  31.3 us
    dynamic_slice x36, local copies, waits for them, and re-layouts, fold_column(): lax.scan(scan_step, state, (key_blocks, value_blocks, place_blocks))  29.8 us
    reduce_sum x12, other arithmetic, merge_block(): new_sum = run_sum * factor + jnp.sum(weights, axis=-1)  27.5 us
    ppermute x6, starting transfers between devices, from_behind(): lax.ppermute(value, axis, [(source, source + steps) for source in range(f...  25.2 us
    all_gather x1, waiting for transfers between devices, body(): lax.all_gather(local_v, 'ctx', axis=0, tiled=True)  21.7 us
  transfers between devices with their start and end apart: 8, of which 2 were waited for; matrix products, arithmetic and copies ran while one was open for 43% of the time, Pallas kernels for 0%

commit v1 on v0

v1 whole, which is shorter than its diff:
```python
import functools
import math

import jax
import jax.numpy as jnp
from jax import lax
from jax.experimental import pallas as pl
from jax.experimental.pallas import tpu as pltpu
from jax.sharding import PartitionSpec as P

HD = 128
KVH = 8
GROUPS = 8
STRETCH = 64
TOK = 128
COL_STRETCHES = 16
REQS = 32
NUM_X = 4
NUM_GRP = 32
ROWS = GROUPS * TOK
TILE = 512
MAX_KEYS = 768

NEG = -1e30
HIDDEN = -2e30
MESH = pl.DeviceIdType.MESH
K, V, POS = 0, 1, 2


def kernel(q_hbm, k_hbm, v_hbm, place_ref, len_ref, out_ref,
           kbuf, vbuf, pbuf, q_vm, qs, acc, run_max, bias,
           local_sem, recv_ici, recv_sib, send_z, send_x, send_fwd, send_sib):
    ctx = lax.axis_index("ctx")
    grp = lax.axis_index("grp")
    x = ctx // 2
    core = ctx % 2
    right = (((x + 1) % NUM_X) * 2 + core, grp)
    left = (((x + NUM_X - 1) % NUM_X) * 2 + core, grp)
    sibling = (x * 2 + 1 - core, grp)
    after = (ctx, (grp + 1) % NUM_GRP)
    before = (ctx, (grp + NUM_GRP - 1) % NUM_GRP)
    bufs = (kbuf, vbuf, pbuf)

    local = [
        pltpu.make_async_copy(k_hbm.at[0], kbuf.at[0, 0, 0], local_sem.at[0]),
        pltpu.make_async_copy(v_hbm.at[0], vbuf.at[0, 0, 0], local_sem.at[1]),
        pltpu.make_async_copy(q_hbm.at[0], q_vm, local_sem.at[2]),
    ]
    for copy in local:
        copy.start()

    first = grp * COL_STRETCHES + place_ref[0, 0]
    second = grp * COL_STRETCHES + place_ref[0, 1]
    end = jnp.int32(0)
    start_first = jnp.int32(0)
    start_second = jnp.int32(0)
    for r in range(REQS):
        end = end + len_ref[r]
        start_first = jnp.where(end <= first, end, start_first)
        start_second = jnp.where(end <= second, end, start_second)

    def by_token(shape, dim, of_first, of_second, step):
        token = lax.broadcasted_iota(jnp.int32, shape, dim)
        within = token % STRETCH
        return jnp.where(token < STRETCH, of_first, of_second) * STRETCH + within * step

    pbuf[0, 0, 0] = by_token((8, TOK), 1, first, second, 1)

    barrier = pltpu.get_barrier_semaphore()
    for device in (right, left, sibling, after, before):
        pl.semaphore_signal(barrier, inc=1, device_id=device, device_id_type=MESH)
    pl.semaphore_wait(barrier, 5)

    started = []

    def send(kind, src, d, rx, side, sem, device):
        recv = (recv_sib if side else recv_ici).at[d, rx, kind]
        copy = pltpu.make_async_remote_copy(
            src_ref=src, dst_ref=bufs[kind].at[d, rx, side],
            send_sem=sem, recv_sem=recv, device_id=device, device_id_type=MESH)
        copy.start()
        started.append(copy)

    def held(kind, d, rx):
        if d == 0 and rx == 0 and kind != POS:
            return (k_hbm, v_hbm)[kind].at[0]
        return bufs[kind].at[d, rx, 0]

    def to_sibling(d, rx, kinds=(POS, K, V)):
        for kind in kinds:
            send(kind, held(kind, d, rx), d, rx, 1, send_sib.at[d, rx, kind], sibling)

    def to_after(d):
        for kind in (POS, K, V):
            send(kind, held(kind, d, 0), d + 1, 0, 0, send_z.at[d, kind], after)

    def along_x(d):
        send(POS, held(POS, d, 0), d, 1, 0, send_x.at[d, 0, POS], right)
        send(POS, held(POS, d, 0), d, 2, 0, send_x.at[d, 1, POS], left)
        send(K, held(K, d, 0), d, 1, 0, send_x.at[d, 0, K], right)
        send(V, held(V, d, 0), d, 2, 0, send_x.at[d, 1, V], left)
        send(V, held(V, d, 0), d, 1, 0, send_x.at[d, 0, V], right)
        send(K, held(K, d, 0), d, 2, 0, send_x.at[d, 1, K], left)

    def forward_x(d):
        send(POS, held(POS, d, 1), d, 3, 0, send_fwd.at[d, POS], right)
        send(K, held(K, d, 1), d, 3, 0, send_fwd.at[d, K], right)
        send(V, held(V, d, 2), d, 3, 0, send_fwd.at[d, V], left)

    def arrived(d, rx, kinds=(POS, K, V), side=0):
        for kind in kinds:
            ref = bufs[kind].at[d, rx, side]
            recv = (recv_sib if side else recv_ici).at[d, rx, kind]
            pltpu.make_async_remote_copy(
                src_ref=ref, dst_ref=ref, send_sem=local_sem.at[3], recv_sem=recv,
                device_id=sibling, device_id_type=MESH).wait_recv()

    def events_first_hop(d):
        arrived(d, 1, (POS, K))
        arrived(d, 2, (POS, V))
        forward_x(d)
        to_sibling(d, 1, (POS, K))
        to_sibling(d, 2, (POS, V))

    def events_rest(d):
        arrived(d, 1, (V,))
        arrived(d, 2, (K,))
        to_sibling(d, 1, (V,))
        to_sibling(d, 2, (K,))

    def events_opposite(d):
        arrived(d, 3)
        to_sibling(d, 3)

    def events_column(d):
        arrived(d, 0)
        if d < 2:
            to_after(d)
        along_x(d)
        to_sibling(d, 0)

    def attend(chunks, is_first=False, is_last=False):
        pieces = [(d, rx, side) for d, rx in chunks for side in range(2)]
        num_keys = TOK * len(pieces)
        key_pos = jnp.concatenate([pbuf[d, rx, side, 0:1, :] for d, rx, side in pieces], axis=1)
        query_pos = by_token((TOK, 1), 0, first, second, 1)
        query_start = by_token((TOK, 1), 0, start_first, start_second, 0)
        visible = (key_pos >= query_start) & (key_pos <= query_pos)
        bias[:, :num_keys] = jnp.where(visible, 0.0, HIDDEN)

        def one_head(head, carry):
            lanes = pl.ds(pl.multiple_of(head * HD, HD), HD)
            keys = jnp.concatenate([kbuf[d, rx, side, :, lanes] for d, rx, side in pieces], axis=0)
            vals = jnp.concatenate([vbuf[d, rx, side, :, lanes] for d, rx, side in pieces], axis=0)
            keys = jnp.concatenate([keys, keys], axis=1)
            vals = jnp.concatenate([vals, jnp.ones_like(vals)], axis=1)
            hidden = bias[:, :num_keys]
            scores = []
            for t in range(ROWS // TILE):
                rows = slice(t * TILE, (t + 1) * TILE)
                scores.append(lax.dot_general(
                    qs[head, rows], keys, (((1,), (1,)), ((), ())),
                    preferred_element_type=jnp.float32))
            for t in range(ROWS // TILE):
                rows = slice(t * TILE, (t + 1) * TILE)
                masked = scores[t].reshape(TILE // TOK, TOK, num_keys) + hidden[None]
                masked = masked.reshape(TILE, num_keys)
                top = jnp.max(masked, axis=1, keepdims=True)
                if not is_first:
                    old = run_max[head, rows]
                    top = jnp.maximum(old[:, 0:1], top)
                weights = jnp.exp2(masked - top).astype(jnp.bfloat16)
                part = lax.dot_general(
                    weights, vals, (((1,), (0,)), ((), ())),
                    preferred_element_type=jnp.float32)
                if not is_first:
                    factor = jnp.exp2(old - top)
                    part = part + acc[head, rows] * jnp.concatenate([factor, factor], axis=1)
                if is_last:
                    result = (part[:, :HD] / part[:, HD:]).astype(jnp.bfloat16)
                    for j in range(TILE // TOK):
                        group = t * (TILE // TOK) + j
                        place = pl.ds(pl.multiple_of((head * GROUPS + group) * HD, HD), HD)
                        out_ref[0, :, place] = result[j * TOK:(j + 1) * TOK]
                else:
                    acc[head, rows] = part
                    run_max[head, rows] = jnp.broadcast_to(top, (TILE, HD))
            return carry

        lax.fori_loop(0, KVH, one_head, 0)

    to_sibling(0, 0)
    to_after(0)
    along_x(0)

    local[2].wait()

    def prepare(head, carry):
        for group in range(GROUPS):
            lanes = pl.ds(pl.multiple_of((head * GROUPS + group) * HD, HD), HD)
            scaled = q_vm[:, lanes].astype(jnp.float32) * (math.log2(math.e) / math.sqrt(HD))
            high = scaled.astype(jnp.bfloat16)
            low = (scaled - high.astype(jnp.float32)).astype(jnp.bfloat16)
            qs[head, group * TOK:(group + 1) * TOK, :HD] = high
            qs[head, group * TOK:(group + 1) * TOK, HD:] = low
        return carry

    lax.fori_loop(0, KVH, prepare, 0)
    local[0].wait()
    local[1].wait()
    arrived(0, 0, side=1)
    attend([(0, 0)], is_first=True)

    events_first_hop(0)
    events_column(1)
    events_rest(0)
    for rx in (1, 2):
        arrived(0, rx, side=1)
    arrived(1, 0, side=1)
    attend([(0, 1), (0, 2), (1, 0)])

    events_opposite(0)
    events_column(2)
    events_first_hop(1)
    arrived(0, 3, side=1)
    arrived(2, 0, side=1)
    attend([(0, 3), (2, 0)])

    events_rest(1)
    for rx in (1, 2):
        arrived(1, rx, side=1)
    attend([(1, 1), (1, 2)])

    events_opposite(1)
    events_first_hop(2)
    arrived(1, 3, side=1)
    attend([(1, 3)])

    events_rest(2)
    for rx in (1, 2):
        arrived(2, rx, side=1)
    attend([(2, 1), (2, 2)])

    events_opposite(2)
    arrived(2, 3, side=1)
    attend([(2, 3)], is_last=True)

    for copy in started:
        copy.wait_send()


def body(queries, keys, values, placement, lengths):
    any_spec = pl.BlockSpec(memory_space=pl.ANY)
    smem = pl.BlockSpec(memory_space=pltpu.SMEM)
    dma = pltpu.SemaphoreType.DMA
    return pl.pallas_call(
        kernel,
        out_shape=jax.ShapeDtypeStruct((1, TOK, KVH * GROUPS * HD), jnp.bfloat16),
        in_specs=[any_spec, any_spec, any_spec, smem, smem],
        out_specs=pl.BlockSpec(memory_space=pltpu.VMEM),
        scratch_shapes=[
            pltpu.VMEM((3, NUM_X, 2, TOK, KVH * HD), jnp.bfloat16),
            pltpu.VMEM((3, NUM_X, 2, TOK, KVH * HD), jnp.bfloat16),
            pltpu.VMEM((3, NUM_X, 2, 8, TOK), jnp.int32),
            pltpu.VMEM((TOK, KVH * GROUPS * HD), jnp.bfloat16),
            pltpu.VMEM((KVH, ROWS, 2 * HD), jnp.bfloat16),
            pltpu.VMEM((KVH, ROWS, 2 * HD), jnp.float32),
            pltpu.VMEM((KVH, ROWS, HD), jnp.float32),
            pltpu.VMEM((TOK, MAX_KEYS), jnp.float32),
            dma((4,)),
            dma((3, NUM_X, 3)),
            dma((3, NUM_X, 3)),
            dma((2, 3)),
            dma((3, 2, 3)),
            dma((3, 3)),
            dma((3, NUM_X, 3)),
        ],
        compiler_params=pltpu.CompilerParams(
            collective_id=0, has_side_effects=True, vmem_limit_bytes=56 * 1024 * 1024),
        cost_estimate=pl.CostEstimate(
            flops=4 * TOK * 64 * 3072 * HD, bytes_accessed=5 * 1024 * 1024,
            transcendentals=TOK * 64 * 3072),
    )(queries, keys, values, placement, lengths)


def solution(mesh):
    in_specs = (
        P("grp", "ctx", None),
        P("grp", "ctx", None),
        P("grp", "ctx", None),
        P("grp", "ctx"),
        P(),
    )
    out_specs = P("grp", "ctx", None)
    return jax.shard_map(body, mesh=mesh, in_specs=in_specs, out_specs=out_specs, check_vma=False)
```

time: 476 us -> 97.7 us (0.21)
  the two profiles are of different devices: /device:TPU:88 before, /device:TPU:1 now
where the time goes in v1:
time: 97.7 us; the launch traced here: 97.5 us
  Pallas kernels  94.4 us (97%)
  local copies, waits for them, and re-layouts  3.1 us (3%)
    pallas_call x1, Pallas kernels, body(): pl.pallas_call(kernel, out_shape=jax.ShapeDtypeStruct((1, TOK, KVH * GROU...  94.4 us
    unnamed x1, local copies, waits for them, and re-layouts  3.1 us

profile of v1, /device:TPU:1, one launch (start us, length us, event | category | flops | bytes accessed | tf_op | source)
XLA Modules:
  0.0 97.5 jit_solution(8665473065124264721)
XLA Ops:
  0.0 94.4 %shard_map.55 = bf16[1,128,8192]{2,1,0:T(8,128)(2,1)} custom-call(bf16[1,128,8192]{2,1,0:T(8,128)(2,1)} %q_hbm.1, bf16[1,128,1024]{2,1,0:T(8,128)(2,1)} %k_hbm.1, bf16[1,128,1024]{2,1,0:T(8,128)(2,1)} %v_hbm.1, s32[1,2]{1,0:T(1,128)} %place_ref.1, s32[32]{0:T(128)} %len_ref.1), custom_call_target="tpu_custom_call" | custom-call | flops 12884901888 | bytes 5242880 | tf_op jit(solution)/shard_map/pallas_call | solution.py:256
  94.4 3.1 %copy.7 = bf16[1,128,8192]{2,1,0:T(8,128)(2,1)} copy(bf16[1,128,8192]{2,1,0:T(8,128)(2,1)} %shard_map.55) | data formatting | bytes 4194304

commit v2 on v1

--- a/solution.py
+++ b/solution.py
@@ -21,14 +21,14 @@
 TILE = 512
 MAX_KEYS = 768
 
-NEG = -1e30
 HIDDEN = -2e30
+SCALE = math.log2(math.e) / math.sqrt(HD)
 MESH = pl.DeviceIdType.MESH
 K, V, POS = 0, 1, 2
 
 
 def kernel(q_hbm, k_hbm, v_hbm, place_ref, len_ref, out_ref,
-           kbuf, vbuf, pbuf, q_vm, qs, acc, run_max, bias,
+           kbuf, vbuf, pbuf, q_vm, qs, acc, run_max, extra,
            local_sem, recv_ici, recv_sib, send_z, send_x, send_fwd, send_sib):
     ctx = lax.axis_index("ctx")
     grp = lax.axis_index("grp")
@@ -59,12 +59,8 @@
         start_first = jnp.where(end <= first, end, start_first)
         start_second = jnp.where(end <= second, end, start_second)
 
-    def by_token(shape, dim, of_first, of_second, step):
-        token = lax.broadcasted_iota(jnp.int32, shape, dim)
-        within = token % STRETCH
-        return jnp.where(token < STRETCH, of_first, of_second) * STRETCH + within * step
-
-    pbuf[0, 0, 0] = by_token((8, TOK), 1, first, second, 1)
+    pbuf[0, 0, 0, 0:8] = jnp.full((8, TOK), first, jnp.int32)
+    pbuf[0, 0, 0, 8:16] = jnp.full((8, TOK), second, jnp.int32)
 
     barrier = pltpu.get_barrier_semaphore()
     for device in (right, left, sibling, after, before):
@@ -139,22 +135,32 @@
         along_x(d)
         to_sibling(d, 0)
 
+    def causal():
+        row = lax.broadcasted_iota(jnp.int32, (TOK, TOK), 0)
+        col = lax.broadcasted_iota(jnp.int32, (TOK, TOK), 1)
+        later = (row // STRETCH == col // STRETCH) & (col > row)
+        return jnp.where(later, HIDDEN, 0.0)
+
     def attend(chunks, is_first=False, is_last=False):
         pieces = [(d, rx, side) for d, rx in chunks for side in range(2)]
         num_keys = TOK * len(pieces)
-        key_pos = jnp.concatenate([pbuf[d, rx, side, 0:1, :] for d, rx, side in pieces], axis=1)
-        query_pos = by_token((TOK, 1), 0, first, second, 1)
-        query_start = by_token((TOK, 1), 0, start_first, start_second, 0)
-        visible = (key_pos >= query_start) & (key_pos <= query_pos)
-        bias[:, :num_keys] = jnp.where(visible, 0.0, HIDDEN)
+        lane = lax.broadcasted_iota(jnp.int32, (8, HD), 1)
+        for i, (d, rx, side) in enumerate(pieces):
+            for half in range(2):
+                stretch = pbuf[d, rx, side, 8 * half:8 * half + 8, :]
+                seen_first = (stretch >= start_first) & (stretch <= first)
+                seen_second = (stretch >= start_second) & (stretch <= second)
+                seen = jnp.where(lane == 0, seen_first.astype(jnp.int32), seen_second.astype(jnp.int32))
+                hide = jnp.where(seen == 1, 0.0, HIDDEN)
+                row = i * TOK + half * STRETCH
+                extra[row:row + STRETCH, :] = jnp.concatenate([hide] * 8, axis=0).astype(jnp.bfloat16)
 
         def one_head(head, carry):
             lanes = pl.ds(pl.multiple_of(head * HD, HD), HD)
             keys = jnp.concatenate([kbuf[d, rx, side, :, lanes] for d, rx, side in pieces], axis=0)
             vals = jnp.concatenate([vbuf[d, rx, side, :, lanes] for d, rx, side in pieces], axis=0)
-            keys = jnp.concatenate([keys, keys], axis=1)
+            keys = jnp.concatenate([keys, extra[:num_keys, :]], axis=1)
             vals = jnp.concatenate([vals, jnp.ones_like(vals)], axis=1)
-            hidden = bias[:, :num_keys]
             scores = []
             for t in range(ROWS // TILE):
                 rows = slice(t * TILE, (t + 1) * TILE)
@@ -163,18 +169,20 @@
                     preferred_element_type=jnp.float32))
             for t in range(ROWS // TILE):
                 rows = slice(t * TILE, (t + 1) * TILE)
-                masked = scores[t].reshape(TILE // TOK, TOK, num_keys) + hidden[None]
-                masked = masked.reshape(TILE, num_keys)
+                masked = scores[t]
+                if is_first:
+                    own = masked[:, :TOK].reshape(TILE // TOK, TOK, TOK) + causal()[None]
+                    masked = jnp.concatenate([own.reshape(TILE, TOK), masked[:, TOK:]], axis=1)
                 top = jnp.max(masked, axis=1, keepdims=True)
                 if not is_first:
                     old = run_max[head, rows]
                     top = jnp.maximum(old[:, 0:1], top)
-                weights = jnp.exp2(masked - top).astype(jnp.bfloat16)
+                weights = jnp.exp2((masked - top) * SCALE).astype(jnp.bfloat16)
                 part = lax.dot_general(
                     weights, vals, (((1,), (0,)), ((), ())),
                     preferred_element_type=jnp.float32)
                 if not is_first:
-                    factor = jnp.exp2(old - top)
+                    factor = jnp.exp2((old - top) * SCALE)
                     part = part + acc[head, rows] * jnp.concatenate([factor, factor], axis=1)
                 if is_last:
                     result = (part[:, :HD] / part[:, HD:]).astype(jnp.bfloat16)
@@ -195,14 +203,15 @@
 
     local[2].wait()
 
+    row = lax.broadcasted_iota(jnp.int32, (TOK, HD), 0)
+    col = lax.broadcasted_iota(jnp.int32, (TOK, HD), 1)
+    which = jnp.where(row // STRETCH == col, 1.0, 0.0).astype(jnp.bfloat16)
+
     def prepare(head, carry):
         for group in range(GROUPS):
             lanes = pl.ds(pl.multiple_of((head * GROUPS + group) * HD, HD), HD)
-            scaled = q_vm[:, lanes].astype(jnp.float32) * (math.log2(math.e) / math.sqrt(HD))
-            high = scaled.astype(jnp.bfloat16)
-            low = (scaled - high.astype(jnp.float32)).astype(jnp.bfloat16)
-            qs[head, group * TOK:(group + 1) * TOK, :HD] = high
-            qs[head, group * TOK:(group + 1) * TOK, HD:] = low
+            qs[head, group * TOK:(group + 1) * TOK, :HD] = q_vm[:, lanes]
+            qs[head, group * TOK:(group + 1) * TOK, HD:] = which
         return carry
 
     lax.fori_loop(0, KVH, prepare, 0)
@@ -261,12 +270,12 @@
         scratch_shapes=[
             pltpu.VMEM((3, NUM_X, 2, TOK, KVH * HD), jnp.bfloat16),
             pltpu.VMEM((3, NUM_X, 2, TOK, KVH * HD), jnp.bfloat16),
-            pltpu.VMEM((3, NUM_X, 2, 8, TOK), jnp.int32),
+            pltpu.VMEM((3, NUM_X, 2, 16, TOK), jnp.int32),
             pltpu.VMEM((TOK, KVH * GROUPS * HD), jnp.bfloat16),
             pltpu.VMEM((KVH, ROWS, 2 * HD), jnp.bfloat16),
             pltpu.VMEM((KVH, ROWS, 2 * HD), jnp.float32),
             pltpu.VMEM((KVH, ROWS, HD), jnp.float32),
-            pltpu.VMEM((TOK, MAX_KEYS), jnp.float32),
+            pltpu.VMEM((MAX_KEYS, HD), jnp.bfloat16),
             dma((4,)),
             dma((3, NUM_X, 3)),
             dma((3, NUM_X, 3)),

time: 97.7 us -> 97.7 us (level)
  no operation moved by 1% of the time
where the time goes in v2:
time: 97.7 us; the launch traced here: 97.5 us
  Pallas kernels  94.4 us (97%)
  local copies, waits for them, and re-layouts  3.1 us (3%)
    pallas_call x1, Pallas kernels, body(): pl.pallas_call(kernel, out_shape=jax.ShapeDtypeStruct((1, TOK, KVH * GROU...  94.4 us
    unnamed x1, local copies, waits for them, and re-layouts  3.1 us

profile of v2, /device:TPU:1, one launch (start us, length us, event | category | flops | bytes accessed | tf_op | source)
XLA Modules:
  0.0 97.5 jit_solution(12884990306414527709)
XLA Ops:
  0.0 94.4 %shard_map.55 = bf16[1,128,8192]{2,1,0:T(8,128)(2,1)} custom-call(bf16[1,128,8192]{2,1,0:T(8,128)(2,1)} %q_hbm.1, bf16[1,128,1024]{2,1,0:T(8,128)(2,1)} %k_hbm.1, bf16[1,128,1024]{2,1,0:T(8,128)(2,1)} %v_hbm.1, s32[1,2]{1,0:T(1,128)} %place_ref.1, s32[32]{0:T(128)} %len_ref.1), custom_call_target="tpu_custom_call" | custom-call | flops 12884901888 | bytes 5242880 | tf_op jit(solution)/shard_map/pallas_call | solution.py:265
  94.5 3.1 %copy.7 = bf16[1,128,8192]{2,1,0:T(8,128)(2,1)} copy(bf16[1,128,8192]{2,1,0:T(8,128)(2,1)} %shard_map.55) | data formatting | bytes 4194304

commit v3 on v2

--- a/solution.py
+++ b/solution.py
@@ -20,6 +20,7 @@
 ROWS = GROUPS * TOK
 TILE = 512
 MAX_KEYS = 768
+HEADS_AT_ONCE = 2
 
 HIDDEN = -2e30
 SCALE = math.log2(math.e) / math.sqrt(HD)
@@ -155,47 +156,60 @@
                 row = i * TOK + half * STRETCH
                 extra[row:row + STRETCH, :] = jnp.concatenate([hide] * 8, axis=0).astype(jnp.bfloat16)
 
-        def one_head(head, carry):
+        def load(head):
             lanes = pl.ds(pl.multiple_of(head * HD, HD), HD)
             keys = jnp.concatenate([kbuf[d, rx, side, :, lanes] for d, rx, side in pieces], axis=0)
             vals = jnp.concatenate([vbuf[d, rx, side, :, lanes] for d, rx, side in pieces], axis=0)
             keys = jnp.concatenate([keys, extra[:num_keys, :]], axis=1)
             vals = jnp.concatenate([vals, jnp.ones_like(vals)], axis=1)
-            scores = []
-            for t in range(ROWS // TILE):
-                rows = slice(t * TILE, (t + 1) * TILE)
-                scores.append(lax.dot_general(
-                    qs[head, rows], keys, (((1,), (1,)), ((), ())),
-                    preferred_element_type=jnp.float32))
-            for t in range(ROWS // TILE):
-                rows = slice(t * TILE, (t + 1) * TILE)
-                masked = scores[t]
-                if is_first:
-                    own = masked[:, :TOK].reshape(TILE // TOK, TOK, TOK) + causal()[None]
-                    masked = jnp.concatenate([own.reshape(TILE, TOK), masked[:, TOK:]], axis=1)
-                top = jnp.max(masked, axis=1, keepdims=True)
-                if not is_first:
-                    old = run_max[head, rows]
-                    top = jnp.maximum(old[:, 0:1], top)
-                weights = jnp.exp2((masked - top) * SCALE).astype(jnp.bfloat16)
-                part = lax.dot_general(
-                    weights, vals, (((1,), (0,)), ((), ())),
-                    preferred_element_type=jnp.float32)
-                if not is_first:
-                    factor = jnp.exp2((old - top) * SCALE)
-                    part = part + acc[head, rows] * jnp.concatenate([factor, factor], axis=1)
-                if is_last:
-                    result = (part[:, :HD] / part[:, HD:]).astype(jnp.bfloat16)
-                    for j in range(TILE // TOK):
-                        group = t * (TILE // TOK) + j
-                        place = pl.ds(pl.multiple_of((head * GROUPS + group) * HD, HD), HD)
-                        out_ref[0, :, place] = result[j * TOK:(j + 1) * TOK]
-                else:
-                    acc[head, rows] = part
-                    run_max[head, rows] = jnp.broadcast_to(top, (TILE, HD))
+            return head, keys, vals
+
+        def score(loaded, rows):
+            head, keys, _ = loaded
+            return lax.dot_general(
+                qs[head, rows], keys, (((1,), (1,)), ((), ())),
+                preferred_element_type=jnp.float32)
+
+        def absorb(loaded, rows, scores):
+            head, _, vals = loaded
+            if is_first:
+                own = scores[:, :TOK].reshape(TILE // TOK, TOK, TOK) + causal()[None]
+                scores = jnp.concatenate([own.reshape(TILE, TOK), scores[:, TOK:]], axis=1)
+            top = jnp.broadcast_to(jnp.max(scores, axis=1, keepdims=True), (TILE, HD)) * SCALE
+            if not is_first:
+                old = run_max[head, rows]
+                top = jnp.maximum(old, top)
+            tops = jnp.concatenate([top] * (num_keys // HD), axis=1)
+            weights = jnp.exp2(scores * SCALE - tops).astype(jnp.bfloat16)
+            part = lax.dot_general(
+                weights, vals, (((1,), (0,)), ((), ())),
+                preferred_element_type=jnp.float32)
+            if not is_first:
+                factor = jnp.exp2(old - top)
+                part = part + acc[head, rows] * jnp.concatenate([factor, factor], axis=1)
+            if is_last:
+                result = (part[:, :HD] / part[:, HD:]).astype(jnp.bfloat16)
+                for j in range(TILE // TOK):
+                    group = rows.start // TOK + j
+                    place = pl.ds(pl.multiple_of((head * GROUPS + group) * HD, HD), HD)
+                    out_ref[0, :, place] = result[j * TOK:(j + 1) * TOK]
+            else:
+                acc[head, rows] = part
+                run_max[head, rows] = top
+
+        def some_heads(step, carry):
+            work = []
+            for i in range(HEADS_AT_ONCE):
+                loaded = load(step * HEADS_AT_ONCE + i)
+                work += [(loaded, slice(t, t + TILE)) for t in range(0, ROWS, TILE)]
+            scores = score(*work[0])
+            for i, (loaded, rows) in enumerate(work):
+                following = score(*work[i + 1]) if i + 1 < len(work) else None
+                absorb(loaded, rows, scores)
+                scores = following
             return carry
 
-        lax.fori_loop(0, KVH, one_head, 0)
+        lax.fori_loop(0, KVH // HEADS_AT_ONCE, some_heads, 0)
 
     to_sibling(0, 0)
     to_after(0)

time: 97.7 us -> 85.8 us (0.88)
  Pallas kernels: 94.4 us -> 82.6 us
    pallas_call x1, Pallas kernels: 94.4 us -> 82.6 us  [body(): pl.pallas_call(kernel, out_shape=jax.ShapeDtypeStruct((1, TOK, KVH * GROU...]
where the time goes in v3:
time: 85.8 us; the launch traced here: 85.7 us
  Pallas kernels  82.6 us (96%)
  local copies, waits for them, and re-layouts  3.1 us (4%)
    pallas_call x1, Pallas kernels, body(): pl.pallas_call(kernel, out_shape=jax.ShapeDtypeStruct((1, TOK, KVH * GROU...  82.6 us
    unnamed x1, local copies, waits for them, and re-layouts  3.1 us

profile of v3, /device:TPU:1, one launch (start us, length us, event | category | flops | bytes accessed | tf_op | source)
XLA Modules:
  0.0 85.7 jit_solution(1559584672092781677)
XLA Ops:
  0.0 82.6 %shard_map.55 = bf16[1,128,8192]{2,1,0:T(8,128)(2,1)} custom-call(bf16[1,128,8192]{2,1,0:T(8,128)(2,1)} %q_hbm.1, bf16[1,128,1024]{2,1,0:T(8,128)(2,1)} %k_hbm.1, bf16[1,128,1024]{2,1,0:T(8,128)(2,1)} %v_hbm.1, s32[1,2]{1,0:T(1,128)} %place_ref.1, s32[32]{0:T(128)} %len_ref.1), custom_call_target="tpu_custom_call" | custom-call | flops 12884901888 | bytes 5242880 | tf_op jit(solution)/shard_map/pallas_call | solution.py:279
  82.6 3.1 %copy.7 = bf16[1,128,8192]{2,1,0:T(8,128)(2,1)} copy(bf16[1,128,8192]{2,1,0:T(8,128)(2,1)} %shard_map.55) | data formatting | bytes 4194304

commit v4 on v3

v4 whole, which is shorter than its diff:
```python
import math

import jax
import jax.numpy as jnp
from jax import lax
from jax.experimental import pallas as pl
from jax.experimental.pallas import tpu as pltpu
from jax.sharding import PartitionSpec as P

HD = 128
KVH = 8
GROUPS = 8
STRETCH = 64
TOK = 128
COL_STRETCHES = 16
REQS = 32
NUM_X = 4
NUM_GRP = 32
ROWS = GROUPS * TOK
TILE = 512
HALF_HEADS = 4
HALF_LANES = HALF_HEADS * HD
HEADS_AT_ONCE = 2
MAX_KEYS = 512
COPY_PARTS = TOK // 16
SUM_ROWS = 16
ACC_ROWS = HD + SUM_ROWS
OUT_LANES = HEADS_AT_ONCE * GROUPS * HD
NUM_OUT = KVH // HEADS_AT_ONCE

HIDDEN = -2e30
SCALE = math.log2(math.e) / math.sqrt(HD)
MESH = pl.DeviceIdType.MESH
H0, H1, POS = 0, 1, 2


def kernel(q_hbm, k_hbm, v_hbm, place_ref, len_ref, out_hbm,
           kvbuf, pbuf, q_vm, out_vm, acc, run_max, extra,
           local_sem, out_sem, recv_ici, recv_sib, send_z, send_x, send_sib):
    ctx = lax.axis_index("ctx")
    grp = lax.axis_index("grp")
    x = ctx // 2
    core = ctx % 2
    right = (((x + 1) % NUM_X) * 2 + core, grp)
    left = (((x + NUM_X - 1) % NUM_X) * 2 + core, grp)
    sibling = (x * 2 + 1 - core, grp)
    after = (ctx, (grp + 1) % NUM_GRP)
    before = (ctx, (grp + NUM_GRP - 1) % NUM_GRP)

    local = []
    for half in range(2):
        lanes = slice(half * HALF_LANES, (half + 1) * HALF_LANES)
        for part, source in enumerate((k_hbm, v_hbm)):
            local.append(pltpu.make_async_copy(
                source.at[0, :, lanes], kvbuf.at[0, 0, 0, half, part], local_sem.at[half, part]))
    queries_in = pltpu.make_async_copy(q_hbm.at[0], q_vm, local_sem.at[2, 0])
    for copy in local + [queries_in]:
        copy.start()

    first = grp * COL_STRETCHES + place_ref[0, 0]
    second = grp * COL_STRETCHES + place_ref[0, 1]
    pbuf[0, 0, 0, 0:8] = jnp.full((8, TOK), first, jnp.int32)
    pbuf[0, 0, 0, 8:16] = jnp.full((8, TOK), second, jnp.int32)

    barrier = pltpu.get_barrier_semaphore()
    for device in (right, left, sibling, after, before):
        pl.semaphore_signal(barrier, inc=1, device_id=device, device_id_type=MESH)
    pl.semaphore_wait(barrier, 5)

    started = []

    def unit(kind, d, rx, side):
        if kind == POS:
            return pbuf.at[d, rx, side]
        return kvbuf.at[d, rx, side, kind]

    def send(kind, src, dst, side, sem, device):
        recv = (recv_sib if side else recv_ici).at[dst[0], dst[1], kind]
        copy = pltpu.make_async_remote_copy(
            src_ref=unit(kind, src[0], src[1], 0), dst_ref=unit(kind, dst[0], dst[1], side),
            send_sem=sem, recv_sem=recv, device_id=device, device_id_type=MESH)
        copy.start()
        started.append(copy)

    def to_sibling(d, rx, kind):
        send(kind, (d, rx), (d, rx), 1, send_sib.at[d, rx, kind], sibling)

    def to_after(d, rx, kind):
        send(kind, (d, rx), (d + 1, rx), 0, send_z.at[d, rx, kind], after)

    def to_right(d, rx, kind):
        target = 1 if rx == 0 else 3
        send(kind, (d, rx), (d, target), 0, send_x.at[d, 0, rx, kind], right)

    def to_left(d, rx, kind):
        target = 2 if rx == 0 else 3
        send(kind, (d, rx), (d, target), 0, send_x.at[d, 1, rx, kind], left)

    waited = set()

    def wait_unit(d, rx, kind, side):
        if (d, rx, kind, side) in waited or (d, rx, side) == (0, 0, 0):
            return
        waited.add((d, rx, kind, side))
        ref = unit(kind, d, rx, side)
        recv = (recv_sib if side else recv_ici).at[d, rx, kind]
        pltpu.make_async_remote_copy(
            src_ref=ref, dst_ref=ref, send_sem=local_sem.at[2, 1], recv_sem=recv,
            device_id=sibling, device_id_type=MESH).wait_recv()

    def got(d, rx, kind):
        if (d, rx, kind, 0) in waited:
            return
        wait_unit(d, rx, kind, 0)
        if rx == 0:
            if d < 2:
                to_after(d, 0, kind)
            if kind == POS:
                to_right(d, 0, POS)
                to_left(d, 0, POS)
            elif kind == H0:
                to_right(d, 0, H0)
            else:
                to_left(d, 0, H1)
                to_right(d, 0, H1)
                to_left(d, 0, H0)
        elif rx == 1 and d != 1 and kind in (POS, H0):
            to_right(d, 1, kind)
        elif rx == 2 and d != 1 and kind == H1:
            to_left(d, 2, kind)
        elif rx == 3 and d == 0:
            to_after(d, 3, kind)
        to_sibling(d, rx, kind)

    row = lax.broadcasted_iota(jnp.int32, (TOK, TOK), 0)
    col = lax.broadcasted_iota(jnp.int32, (TOK, TOK), 1)
    which = jnp.where(row // STRETCH == col, 1.0, 0.0).astype(jnp.bfloat16)
    which = jnp.concatenate([which] * (TILE // TOK), axis=0)
    eye = jnp.where(row == col, 1.0, 0.0).astype(jnp.bfloat16)

    def causal():
        later = (row // STRETCH == col // STRETCH) & (row > col)
        hide = jnp.where(later, HIDDEN, 0.0)
        return jnp.concatenate([hide] * (TILE // TOK), axis=1)

    def swapped(a, b):
        return lax.dot_general(a, b, (((1,), (1,)), ((), ())), preferred_element_type=jnp.float32)

    def attend(chunks, halves=(H0, H1), is_first=False, is_last=False):
        for d, rx in chunks:
            for kind in (POS,) + halves:
                got(d, rx, kind)
        for d, rx in chunks:
            for kind in (POS,) + halves:
                wait_unit(d, rx, kind, 1)
        pieces = [(d, rx, side) for d, rx in chunks for side in range(2)]
        num_keys = TOK * len(pieces)
        lane = lax.broadcasted_iota(jnp.int32, (8, HD), 1)
        for i, (d, rx, side) in enumerate(pieces):
            for half in range(2):
                stretch = pbuf[d, rx, side, 8 * half:8 * half + 8, :]
                seen_first = (stretch >= start_first) & (stretch <= first)
                seen_second = (stretch >= start_second) & (stretch <= second)
                seen = jnp.where(lane == 0, seen_first.astype(jnp.int32), seen_second.astype(jnp.int32))
                hide = jnp.where(seen == 1, 0.0, HIDDEN)
                at = i * TOK + half * STRETCH
                extra[at:at + STRETCH, :] = jnp.concatenate([hide] * 8, axis=0).astype(jnp.bfloat16)

        def load(half, inner):
            lanes = pl.ds(pl.multiple_of(inner * HD, HD), HD)
            keys = jnp.concatenate(
                [kvbuf[d, rx, side, half, 0, :, lanes] for d, rx, side in pieces], axis=0)
            vals = jnp.concatenate(
                [kvbuf[d, rx, side, half, 1, :, lanes] for d, rx, side in pieces], axis=0)
            keys = jnp.concatenate([keys, extra[:num_keys, :]], axis=1)
            vals = swapped(eye, vals).astype(jnp.bfloat16)
            vals = jnp.concatenate([vals, jnp.ones((SUM_ROWS, num_keys), jnp.bfloat16)], axis=0)
            return half * HALF_HEADS + inner, keys, vals

        def score(loaded, tile):
            head, keys, _ = loaded
            queries = []
            for j in range(TILE // TOK):
                group = tile * (TILE // TOK) + j
                lanes = pl.ds(pl.multiple_of((head * GROUPS + group) * HD, HD), HD)
                queries.append(q_vm[:, lanes])
            queries = jnp.concatenate([jnp.concatenate(queries, axis=0), which], axis=1)
            return swapped(keys, queries)

        def absorb(loaded, tile, scores):
            head, _, vals = loaded
            rows = slice(tile * TILE, (tile + 1) * TILE)
            if is_first:
                scores = jnp.concatenate([scores[:TOK] + causal(), scores[TOK:]], axis=0)
            scores = scores.reshape(num_keys // 8, 8, TILE)
            top = jnp.max(jnp.max(scores, axis=0), axis=0, keepdims=True) * SCALE
            top = jnp.broadcast_to(top, (8, TILE))
            if not is_first:
                old = run_max[head, :, rows]
                top = jnp.maximum(old, top)
            weights = jnp.exp2(scores * SCALE - top[None])
            weights = weights.reshape(num_keys, TILE).astype(jnp.bfloat16)
            part = lax.dot_general(
                vals, weights, (((1,), (0,)), ((), ())), preferred_element_type=jnp.float32)
            part = part.reshape(ACC_ROWS // 8, 8, TILE)
            if not is_first:
                factor = jnp.exp2(old - top)
                part = part + acc[head, :, rows].reshape(ACC_ROWS // 8, 8, TILE) * factor[None]
            if is_last:
                inverse = 1.0 / part[HD // 8]
                result = (part[:HD // 8] * inverse[None]).reshape(HD, TILE).astype(jnp.bfloat16)
                for j in range(TILE // TOK):
                    group = tile * (TILE // TOK) + j
                    place = pl.ds(pl.multiple_of((head * GROUPS + group) * HD, HD), HD)
                    turned = swapped(eye, result[:, j * TOK:(j + 1) * TOK])
                    out_vm[:, place] = turned.astype(jnp.bfloat16)
            else:
                acc[head, :, rows] = part.reshape(ACC_ROWS, TILE)
                run_max[head, :, rows] = top

        steps = HALF_HEADS // HEADS_AT_ONCE

        def some_heads(step, carry):
            half = halves[0] if len(halves) == 1 else step // steps
            work = []
            for i in range(HEADS_AT_ONCE):
                loaded = load(half, (step % steps) * HEADS_AT_ONCE + i)
                work += [(loaded, tile) for tile in range(ROWS // TILE)]
            scores = score(*work[0])
            for i, (loaded, tile) in enumerate(work):
                following = score(*work[i + 1]) if i + 1 < len(work) else None
                absorb(loaded, tile, scores)
                scores = following
            if is_last:
                output(step).start()
            return carry

        lax.fori_loop(0, steps * len(halves), some_heads, 0)

    def output(step):
        lanes = pl.ds(pl.multiple_of(step * OUT_LANES, OUT_LANES), OUT_LANES)
        return pltpu.make_async_copy(out_vm.at[:, lanes], out_hbm.at[0, :, lanes], out_sem.at[step])

    for device in (to_sibling, to_after, to_right, to_left):
        device(0, 0, POS)
    local[0].wait()
    local[1].wait()
    to_right(0, 0, H0)
    to_sibling(0, 0, H0)
    to_after(0, 0, H0)
    local[2].wait()
    local[3].wait()
    to_left(0, 0, H1)
    to_sibling(0, 0, H1)
    to_after(0, 0, H1)
    to_right(0, 0, H1)
    to_left(0, 0, H0)
    for kind in (POS, H0, H1):
        waited.add((0, 0, kind, 0))

    end = jnp.int32(0)
    start_first = jnp.int32(0)
    start_second = jnp.int32(0)
    for r in range(REQS):
        end = end + len_ref[r]
        start_first = jnp.where(end <= first, end, start_first)
        start_second = jnp.where(end <= second, end, start_second)

    queries_in.wait()
    attend([(0, 0)], is_first=True)

    got(0, 1, POS)
    got(0, 1, H0)
    got(0, 2, H1)
    got(1, 0, POS)
    got(1, 0, H0)
    attend([(0, 1)], (H0,))
    attend([(0, 2)], (H1,))
    got(1, 0, H1)
    attend([(0, 1), (1, 0)], (H1,))
    attend([(0, 2), (1, 0)], (H0,))
    for kind in (POS, H0, H1):
        got(0, 3, kind)
    got(2, 0, POS)
    got(2, 0, H0)
    attend([(0, 3)])
    got(2, 0, H1)
    attend([(2, 0), (1, 1)], (H0,))
    attend([(2, 0), (1, 2)], (H1,))
    got(1, 1, H1)
    got(1, 2, H0)
    attend([(1, 1), (1, 3)], (H1,))
    got(2, 1, POS)
    got(2, 1, H0)
    got(2, 2, H1)
    attend([(1, 2), (1, 3)], (H0,))
    attend([(2, 1), (2, 2)])
    attend([(2, 3)], is_last=True)

    for step in range(NUM_OUT):
        output(step).wait()
    for copy in started:
        copy.wait_send()


def copy_kernel(source, target, held, sems):
    parts = []
    for part in range(COPY_PARTS):
        rows = slice(part * 16, (part + 1) * 16)
        parts.append((
            pltpu.make_async_copy(source.at[0, rows], held.at[rows], sems.at[0, part]),
            pltpu.make_async_copy(held.at[rows], target.at[0, rows], sems.at[1, part])))
    for come, _ in parts:
        come.start()
    for come, leave in parts:
        come.wait()
        leave.start()
    for _, leave in parts:
        leave.wait()


def body(queries, keys, values, placement, lengths):
    any_spec = pl.BlockSpec(memory_space=pl.ANY)
    smem = pl.BlockSpec(memory_space=pltpu.SMEM)
    dma = pltpu.SemaphoreType.DMA
    out_shape = jax.ShapeDtypeStruct((1, TOK, KVH * GROUPS * HD), jnp.bfloat16)
    result = pl.pallas_call(
        kernel,
        out_shape=out_shape,
        in_specs=[any_spec, any_spec, any_spec, smem, smem],
        out_specs=any_spec,
        scratch_shapes=[
            pltpu.VMEM((3, NUM_X, 2, 2, 2, TOK, HALF_LANES), jnp.bfloat16),
            pltpu.VMEM((3, NUM_X, 2, 16, TOK), jnp.int32),
            pltpu.VMEM((TOK, KVH * GROUPS * HD), jnp.bfloat16),
            pltpu.VMEM((TOK, KVH * GROUPS * HD), jnp.bfloat16),
            pltpu.VMEM((KVH, ACC_ROWS, ROWS), jnp.float32),
            pltpu.VMEM((KVH, 8, ROWS), jnp.float32),
            pltpu.VMEM((MAX_KEYS, HD), jnp.bfloat16),
            dma((3, 2)),
            dma((NUM_OUT,)),
            dma((3, NUM_X, 3)),
            dma((3, NUM_X, 3)),
            dma((2, NUM_X, 3)),
            dma((3, 2, 3, 3)),
            dma((3, NUM_X, 3)),
        ],
        compiler_params=pltpu.CompilerParams(
            collective_id=0, has_side_effects=True, vmem_limit_bytes=56 * 1024 * 1024),
        cost_estimate=pl.CostEstimate(
            flops=4 * TOK * 64 * 3072 * HD, bytes_accessed=5 * 1024 * 1024,
            transcendentals=TOK * 64 * 3072),
    )(queries, keys, values, placement, lengths)
    return pl.pallas_call(
        copy_kernel,
        out_shape=out_shape,
        in_specs=[any_spec],
        out_specs=any_spec,
        scratch_shapes=[
            pltpu.VMEM((TOK, KVH * GROUPS * HD), jnp.bfloat16),
            dma((2, COPY_PARTS)),
        ],
        compiler_params=pltpu.CompilerParams(vmem_limit_bytes=56 * 1024 * 1024),
    )(result)


def solution(mesh):
    in_specs = (
        P("grp", "ctx", None),
        P("grp", "ctx", None),
        P("grp", "ctx", None),
        P("grp", "ctx"),
        P(),
    )
    out_specs = P("grp", "ctx", None)
    return jax.shard_map(body, mesh=mesh, in_specs=in_specs, out_specs=out_specs, check_vma=False)
```

time: 85.8 us -> 91.6 us (1.068)
  Pallas kernels: 82.6 us -> 91.3 us
  local copies, waits for them, and re-layouts: 3.1 us -> 0 us
    pallas_call x1 -> x2, Pallas kernels: 82.6 us -> 91.3 us  [the longest x1 88.9 us: body(): pl.pallas_call(kernel, out_shape=out_shape, in_specs=[any_spec, any_spec,...]
    unnamed x1 -> x0, local copies, waits for them, and re-layouts: 3.1 us -> none
where the time goes in v4:
time: 91.6 us; the launch traced here: 91.5 us
  Pallas kernels  91.3 us (100%)
    pallas_call x1, Pallas kernels, body(): pl.pallas_call(kernel, out_shape=out_shape, in_specs=[any_spec, any_spec,...  88.9 us
    pallas_call x1, Pallas kernels, body(): pl.pallas_call(copy_kernel, out_shape=out_shape, in_specs=[any_spec], out...  2.4 us

profile of v4, /device:TPU:1, one launch (start us, length us, event | category | flops | bytes accessed | tf_op | source)
XLA Modules:
  0.0 91.5 jit_solution(4361153700322597818)
XLA Ops:
  0.0 88.9 %shard_map.55.source = bf16[1,128,8192]{2,1,0:T(8,128)(2,1)} custom-call(bf16[1,128,8192]{2,1,0:T(8,128)(2,1)} %q_hbm.1, bf16[1,128,1024]{2,1,0:T(8,128)(2,1)} %k_hbm.1, bf16[1,128,1024]{2,1,0:T(8,128)(2,1)} %v_hbm.1, s32[1,2]{1,0:T(1,128)} %place_ref.1, s32[32]{0:T(128)} %len_ref.1), custom_call_target="tpu_custom_call" | custom-call | flops 12884901888 | bytes 5242880 | tf_op jit(solution)/shard_map/pallas_call | solution.py:327
  88.9 2.4 %shard_map.56 = bf16[1,128,8192]{2,1,0:T(8,128)(2,1)} custom-call(bf16[1,128,8192]{2,1,0:T(8,128)(2,1)} %shard_map.55.source), custom_call_target="tpu_custom_call" | custom-call | tf_op jit(solution)/shard_map/pallas_call | solution.py:354

commit v5 on v4

--- a/solution.py
+++ b/solution.py
@@ -17,14 +17,12 @@
 NUM_X = 4
 NUM_GRP = 32
 ROWS = GROUPS * TOK
-TILE = 512
+TILE = GROUPS * STRETCH
 HALF_HEADS = 4
 HALF_LANES = HALF_HEADS * HD
 HEADS_AT_ONCE = 2
 MAX_KEYS = 512
 COPY_PARTS = TOK // 16
-SUM_ROWS = 16
-ACC_ROWS = HD + SUM_ROWS
 OUT_LANES = HEADS_AT_ONCE * GROUPS * HD
 NUM_OUT = KVH // HEADS_AT_ONCE
 
@@ -35,7 +33,7 @@
 
 
 def kernel(q_hbm, k_hbm, v_hbm, place_ref, len_ref, out_hbm,
-           kvbuf, pbuf, q_vm, out_vm, acc, run_max, extra,
+           kvbuf, pbuf, q_vm, out_vm, acc, run_max, run_sum, hide,
            local_sem, out_sem, recv_ici, recv_sib, send_z, send_x, send_sib):
     ctx = lax.axis_index("ctx")
     grp = lax.axis_index("grp")
@@ -132,16 +130,11 @@
             to_after(d, 3, kind)
         to_sibling(d, rx, kind)
 
-    row = lax.broadcasted_iota(jnp.int32, (TOK, TOK), 0)
-    col = lax.broadcasted_iota(jnp.int32, (TOK, TOK), 1)
-    which = jnp.where(row // STRETCH == col, 1.0, 0.0).astype(jnp.bfloat16)
-    which = jnp.concatenate([which] * (TILE // TOK), axis=0)
-    eye = jnp.where(row == col, 1.0, 0.0).astype(jnp.bfloat16)
-
-    def causal():
-        later = (row // STRETCH == col // STRETCH) & (row > col)
-        hide = jnp.where(later, HIDDEN, 0.0)
-        return jnp.concatenate([hide] * (TILE // TOK), axis=1)
+    def causal(t):
+        row = lax.broadcasted_iota(jnp.int32, (STRETCH, TOK), 0)
+        col = lax.broadcasted_iota(jnp.int32, (STRETCH, TOK), 1)
+        later = (col // STRETCH == t) & (col % STRETCH > row)
+        return jnp.where(later, HIDDEN, 0.0)
 
     def swapped(a, b):
         return lax.dot_general(a, b, (((1,), (1,)), ((), ())), preferred_element_type=jnp.float32)
@@ -155,16 +148,12 @@
                 wait_unit(d, rx, kind, 1)
         pieces = [(d, rx, side) for d, rx in chunks for side in range(2)]
         num_keys = TOK * len(pieces)
-        lane = lax.broadcasted_iota(jnp.int32, (8, HD), 1)
+        lane = lax.broadcasted_iota(jnp.int32, (8, TOK), 1)
         for i, (d, rx, side) in enumerate(pieces):
-            for half in range(2):
-                stretch = pbuf[d, rx, side, 8 * half:8 * half + 8, :]
-                seen_first = (stretch >= start_first) & (stretch <= first)
-                seen_second = (stretch >= start_second) & (stretch <= second)
-                seen = jnp.where(lane == 0, seen_first.astype(jnp.int32), seen_second.astype(jnp.int32))
-                hide = jnp.where(seen == 1, 0.0, HIDDEN)
-                at = i * TOK + half * STRETCH
-                extra[at:at + STRETCH, :] = jnp.concatenate([hide] * 8, axis=0).astype(jnp.bfloat16)
+            stretch = jnp.where(lane < STRETCH, pbuf[d, rx, side, 0:8, :], pbuf[d, rx, side, 8:16, :])
+            for t, (low, high) in enumerate(((start_first, first), (start_second, second))):
+                seen = (stretch >= low) & (stretch <= high)
+                hide[t, :, i * TOK:(i + 1) * TOK] = jnp.where(seen, 0.0, HIDDEN)
 
         def load(half, inner):
             lanes = pl.ds(pl.multiple_of(inner * HD, HD), HD)
@@ -172,64 +161,65 @@
                 [kvbuf[d, rx, side, half, 0, :, lanes] for d, rx, side in pieces], axis=0)
             vals = jnp.concatenate(
                 [kvbuf[d, rx, side, half, 1, :, lanes] for d, rx, side in pieces], axis=0)
-            keys = jnp.concatenate([keys, extra[:num_keys, :]], axis=1)
-            vals = swapped(eye, vals).astype(jnp.bfloat16)
-            vals = jnp.concatenate([vals, jnp.ones((SUM_ROWS, num_keys), jnp.bfloat16)], axis=0)
             return half * HALF_HEADS + inner, keys, vals
 
-        def score(loaded, tile):
+        def score(loaded):
             head, keys, _ = loaded
             queries = []
-            for j in range(TILE // TOK):
-                group = tile * (TILE // TOK) + j
-                lanes = pl.ds(pl.multiple_of((head * GROUPS + group) * HD, HD), HD)
-                queries.append(q_vm[:, lanes])
-            queries = jnp.concatenate([jnp.concatenate(queries, axis=0), which], axis=1)
-            return swapped(keys, queries)
-
-        def absorb(loaded, tile, scores):
+            for t in range(2):
+                for group in range(GROUPS):
+                    lanes = pl.ds(pl.multiple_of((head * GROUPS + group) * HD, HD), HD)
+                    queries.append(q_vm[t * STRETCH:(t + 1) * STRETCH, lanes])
+            return swapped(jnp.concatenate(queries, axis=0), keys)
+
+        def absorb(loaded, scores):
             head, _, vals = loaded
-            rows = slice(tile * TILE, (tile + 1) * TILE)
-            if is_first:
-                scores = jnp.concatenate([scores[:TOK] + causal(), scores[TOK:]], axis=0)
-            scores = scores.reshape(num_keys // 8, 8, TILE)
-            top = jnp.max(jnp.max(scores, axis=0), axis=0, keepdims=True) * SCALE
-            top = jnp.broadcast_to(top, (8, TILE))
+            masked = []
+            for t in range(2):
+                part = scores[t * TILE:(t + 1) * TILE]
+                if is_first:
+                    own = part[:, :TOK].reshape(GROUPS, STRETCH, TOK) + causal(t)[None]
+                    part = jnp.concatenate([own.reshape(TILE, TOK), part[:, TOK:]], axis=1)
+                part = part.reshape(TILE // 8, 8, num_keys) + hide[t, :, :num_keys][None]
+                masked.append(part.reshape(TILE, num_keys))
+            masked = jnp.concatenate(masked, axis=0)
+            top = jnp.broadcast_to(jnp.max(masked, axis=1, keepdims=True), (ROWS, HD)) * SCALE
             if not is_first:
-                old = run_max[head, :, rows]
+                old = run_max[head]
                 top = jnp.maximum(old, top)
-            weights = jnp.exp2(scores * SCALE - top[None])
-            weights = weights.reshape(num_keys, TILE).astype(jnp.bfloat16)
+            tops = jnp.concatenate([top] * (num_keys // HD), axis=1)
+            weights = jnp.exp2(masked * SCALE - tops)
+            total = weights[:, :HD]
+            for j in range(1, num_keys // HD):
+                total = total + weights[:, j * HD:(j + 1) * HD]
             part = lax.dot_general(
-                vals, weights, (((1,), (0,)), ((), ())), preferred_element_type=jnp.float32)
-            part = part.reshape(ACC_ROWS // 8, 8, TILE)
+                weights.astype(jnp.bfloat16), vals, (((1,), (0,)), ((), ())),
+                preferred_element_type=jnp.float32)
             if not is_first:
                 factor = jnp.exp2(old - top)
-                part = part + acc[head, :, rows].reshape(ACC_ROWS // 8, 8, TILE) * factor[None]
+                part = part + acc[head] * factor
+                total = total + run_sum[head] * factor
             if is_last:
-                inverse = 1.0 / part[HD // 8]
-                result = (part[:HD // 8] * inverse[None]).reshape(HD, TILE).astype(jnp.bfloat16)
-                for j in range(TILE // TOK):
-                    group = tile * (TILE // TOK) + j
-                    place = pl.ds(pl.multiple_of((head * GROUPS + group) * HD, HD), HD)
-                    turned = swapped(eye, result[:, j * TOK:(j + 1) * TOK])
-                    out_vm[:, place] = turned.astype(jnp.bfloat16)
+                result = (part / jnp.sum(total, axis=1, keepdims=True)).astype(jnp.bfloat16)
+                for t in range(2):
+                    for group in range(GROUPS):
+                        place = pl.ds(pl.multiple_of((head * GROUPS + group) * HD, HD), HD)
+                        at = (t * GROUPS + group) * STRETCH
+                        out_vm[t * STRETCH:(t + 1) * STRETCH, place] = result[at:at + STRETCH]
             else:
-                acc[head, :, rows] = part.reshape(ACC_ROWS, TILE)
-                run_max[head, :, rows] = top
+                acc[head] = part
+                run_sum[head] = total
+                run_max[head] = top
 
         steps = HALF_HEADS // HEADS_AT_ONCE
 
         def some_heads(step, carry):
             half = halves[0] if len(halves) == 1 else step // steps
-            work = []
-            for i in range(HEADS_AT_ONCE):
-                loaded = load(half, (step % steps) * HEADS_AT_ONCE + i)
-                work += [(loaded, tile) for tile in range(ROWS // TILE)]
-            scores = score(*work[0])
-            for i, (loaded, tile) in enumerate(work):
-                following = score(*work[i + 1]) if i + 1 < len(work) else None
-                absorb(loaded, tile, scores)
+            work = [load(half, (step % steps) * HEADS_AT_ONCE + i) for i in range(HEADS_AT_ONCE)]
+            scores = score(work[0])
+            for i, loaded in enumerate(work):
+                following = score(work[i + 1]) if i + 1 < len(work) else None
+                absorb(loaded, scores)
                 scores = following
             if is_last:
                 output(step).start()
@@ -334,9 +324,10 @@
             pltpu.VMEM((3, NUM_X, 2, 16, TOK), jnp.int32),
             pltpu.VMEM((TOK, KVH * GROUPS * HD), jnp.bfloat16),
             pltpu.VMEM((TOK, KVH * GROUPS * HD), jnp.bfloat16),
-            pltpu.VMEM((KVH, ACC_ROWS, ROWS), jnp.float32),
-            pltpu.VMEM((KVH, 8, ROWS), jnp.float32),
-            pltpu.VMEM((MAX_KEYS, HD), jnp.bfloat16),
+            pltpu.VMEM((KVH, ROWS, HD), jnp.float32),
+            pltpu.VMEM((KVH, ROWS, HD), jnp.float32),
+            pltpu.VMEM((KVH, ROWS, HD), jnp.float32),
+            pltpu.VMEM((2, 8, MAX_KEYS), jnp.float32),
             dma((3, 2)),
             dma((NUM_OUT,)),
             dma((3, NUM_X, 3)),

time: 91.6 us -> 87.9 us (0.960)
  Pallas kernels: 91.3 us -> 87.6 us
    pallas_call x1, Pallas kernels: 88.9 us -> 85.2 us  [body(): pl.pallas_call(kernel, out_shape=out_shape, in_specs=[any_spec, any_spec,...]
where the time goes in v5:
time: 87.9 us; the launch traced here: 87.8 us
  Pallas kernels  87.6 us (100%)
    pallas_call x1, Pallas kernels, body(): pl.pallas_call(kernel, out_shape=out_shape, in_specs=[any_spec, any_spec,...  85.2 us
    pallas_call x1, Pallas kernels, body(): pl.pallas_call(copy_kernel, out_shape=out_shape, in_specs=[any_spec], out...  2.4 us

profile of v5, /device:TPU:1, one launch (start us, length us, event | category | flops | bytes accessed | tf_op | source)
XLA Modules:
  0.0 87.8 jit_solution(4504058269230744111)
XLA Ops:
  0.0 85.2 %shard_map.55.source = bf16[1,128,8192]{2,1,0:T(8,128)(2,1)} custom-call(bf16[1,128,8192]{2,1,0:T(8,128)(2,1)} %q_hbm.1, bf16[1,128,1024]{2,1,0:T(8,128)(2,1)} %k_hbm.1, bf16[1,128,1024]{2,1,0:T(8,128)(2,1)} %v_hbm.1, s32[1,2]{1,0:T(1,128)} %place_ref.1, s32[32]{0:T(128)} %len_ref.1), custom_call_target="tpu_custom_call" | custom-call | flops 12884901888 | bytes 5242880 | tf_op jit(solution)/shard_map/pallas_call | solution.py:317
  85.2 2.4 %shard_map.56 = bf16[1,128,8192]{2,1,0:T(8,128)(2,1)} custom-call(bf16[1,128,8192]{2,1,0:T(8,128)(2,1)} %shard_map.55.source), custom_call_target="tpu_custom_call" | custom-call | tf_op jit(solution)/shard_map/pallas_call | solution.py:345

commit v6 on v4

--- a/solution.py
+++ b/solution.py
@@ -23,8 +23,7 @@
 HEADS_AT_ONCE = 2
 MAX_KEYS = 512
 COPY_PARTS = TOK // 16
-SUM_ROWS = 16
-ACC_ROWS = HD + SUM_ROWS
+BLOCK = 32
 OUT_LANES = HEADS_AT_ONCE * GROUPS * HD
 NUM_OUT = KVH // HEADS_AT_ONCE
 
@@ -35,7 +34,7 @@
 
 
 def kernel(q_hbm, k_hbm, v_hbm, place_ref, len_ref, out_hbm,
-           kvbuf, pbuf, q_vm, out_vm, acc, run_max, extra,
+           kvbuf, pbuf, q_vm, out_vm, acc, run_max, extra, s_buf, p_buf, f_buf,
            local_sem, out_sem, recv_ici, recv_sib, send_z, send_x, send_sib):
     ctx = lax.axis_index("ctx")
     grp = lax.axis_index("grp")
@@ -132,19 +131,16 @@
             to_after(d, 3, kind)
         to_sibling(d, rx, kind)
 
-    row = lax.broadcasted_iota(jnp.int32, (TOK, TOK), 0)
-    col = lax.broadcasted_iota(jnp.int32, (TOK, TOK), 1)
+    def causal(start):
+        row = lax.broadcasted_iota(jnp.int32, (BLOCK, TOK), 0) + start
+        col = lax.broadcasted_iota(jnp.int32, (BLOCK, TOK), 1)
+        later = (row // STRETCH == col // STRETCH) & (col > row)
+        return jnp.where(later, HIDDEN, 0.0)
+
+    row = lax.broadcasted_iota(jnp.int32, (TOK, HD), 0)
+    col = lax.broadcasted_iota(jnp.int32, (TOK, HD), 1)
     which = jnp.where(row // STRETCH == col, 1.0, 0.0).astype(jnp.bfloat16)
     which = jnp.concatenate([which] * (TILE // TOK), axis=0)
-    eye = jnp.where(row == col, 1.0, 0.0).astype(jnp.bfloat16)
-
-    def causal():
-        later = (row // STRETCH == col // STRETCH) & (row > col)
-        hide = jnp.where(later, HIDDEN, 0.0)
-        return jnp.concatenate([hide] * (TILE // TOK), axis=1)
-
-    def swapped(a, b):
-        return lax.dot_general(a, b, (((1,), (1,)), ((), ())), preferred_element_type=jnp.float32)
 
     def attend(chunks, halves=(H0, H1), is_first=False, is_last=False):
         for d, rx in chunks:
@@ -173,8 +169,7 @@
             vals = jnp.concatenate(
                 [kvbuf[d, rx, side, half, 1, :, lanes] for d, rx, side in pieces], axis=0)
             keys = jnp.concatenate([keys, extra[:num_keys, :]], axis=1)
-            vals = swapped(eye, vals).astype(jnp.bfloat16)
-            vals = jnp.concatenate([vals, jnp.ones((SUM_ROWS, num_keys), jnp.bfloat16)], axis=0)
+            vals = jnp.concatenate([vals, jnp.ones_like(vals)], axis=1)
             return half * HALF_HEADS + inner, keys, vals
 
         def score(loaded, tile):
@@ -185,38 +180,46 @@
                 lanes = pl.ds(pl.multiple_of((head * GROUPS + group) * HD, HD), HD)
                 queries.append(q_vm[:, lanes])
             queries = jnp.concatenate([jnp.concatenate(queries, axis=0), which], axis=1)
-            return swapped(keys, queries)
-
-        def absorb(loaded, tile, scores):
+            return lax.dot_general(
+                queries, keys, (((1,), (1,)), ((), ())), preferred_element_type=jnp.float32)
+
+        def absorb(loaded, tile, slot):
             head, _, vals = loaded
-            rows = slice(tile * TILE, (tile + 1) * TILE)
-            if is_first:
-                scores = jnp.concatenate([scores[:TOK] + causal(), scores[TOK:]], axis=0)
-            scores = scores.reshape(num_keys // 8, 8, TILE)
-            top = jnp.max(jnp.max(scores, axis=0), axis=0, keepdims=True) * SCALE
-            top = jnp.broadcast_to(top, (8, TILE))
-            if not is_first:
-                old = run_max[head, :, rows]
-                top = jnp.maximum(old, top)
-            weights = jnp.exp2(scores * SCALE - top[None])
-            weights = weights.reshape(num_keys, TILE).astype(jnp.bfloat16)
+            first_row = tile * TILE
+            for at in range(0, TILE, BLOCK):
+                rows = slice(first_row + at, first_row + at + BLOCK)
+                block = s_buf[slot, at:at + BLOCK, :num_keys]
+                if is_first:
+                    own = block[:, :TOK] + causal(at % TOK)
+                    s_buf[slot, at:at + BLOCK, :TOK] = own
+                    block = jnp.concatenate([own, block[:, TOK:]], axis=1)
+                top = jnp.broadcast_to(jnp.max(block, axis=1, keepdims=True), (BLOCK, HD)) * SCALE
+                if not is_first:
+                    old = run_max[head, rows]
+                    top = jnp.maximum(old, top)
+                    f_buf[slot, at:at + BLOCK] = jnp.exp2(old - top)
+                run_max[head, rows] = top
+            for at in range(0, TILE, BLOCK):
+                top = run_max[head, first_row + at:first_row + at + BLOCK]
+                for j in range(0, num_keys, HD):
+                    weights = jnp.exp2(s_buf[slot, at:at + BLOCK, j:j + HD] * SCALE - top)
+                    p_buf[slot, at:at + BLOCK, j:j + HD] = weights.astype(jnp.bfloat16)
             part = lax.dot_general(
-                vals, weights, (((1,), (0,)), ((), ())), preferred_element_type=jnp.float32)
-            part = part.reshape(ACC_ROWS // 8, 8, TILE)
-            if not is_first:
-                factor = jnp.exp2(old - top)
-                part = part + acc[head, :, rows].reshape(ACC_ROWS // 8, 8, TILE) * factor[None]
-            if is_last:
-                inverse = 1.0 / part[HD // 8]
-                result = (part[:HD // 8] * inverse[None]).reshape(HD, TILE).astype(jnp.bfloat16)
-                for j in range(TILE // TOK):
-                    group = tile * (TILE // TOK) + j
+                p_buf[slot, :, :num_keys], vals, (((1,), (0,)), ((), ())),
+                preferred_element_type=jnp.float32)
+            for at in range(0, TILE, BLOCK):
+                rows = slice(first_row + at, first_row + at + BLOCK)
+                block = part[at:at + BLOCK]
+                if not is_first:
+                    factor = f_buf[slot, at:at + BLOCK]
+                    block = block + acc[head, rows] * jnp.concatenate([factor, factor], axis=1)
+                if is_last:
+                    group = (first_row + at) // TOK
                     place = pl.ds(pl.multiple_of((head * GROUPS + group) * HD, HD), HD)
-                    turned = swapped(eye, result[:, j * TOK:(j + 1) * TOK])
-                    out_vm[:, place] = turned.astype(jnp.bfloat16)
-            else:
-                acc[head, :, rows] = part.reshape(ACC_ROWS, TILE)
-                run_max[head, :, rows] = top
+                    result = (block[:, :HD] / block[:, HD:]).astype(jnp.bfloat16)
+                    out_vm[at % TOK:at % TOK + BLOCK, place] = result
+                else:
+                    acc[head, rows] = block
 
         steps = HALF_HEADS // HEADS_AT_ONCE
 
@@ -226,11 +229,11 @@
             for i in range(HEADS_AT_ONCE):
                 loaded = load(half, (step % steps) * HEADS_AT_ONCE + i)
                 work += [(loaded, tile) for tile in range(ROWS // TILE)]
-            scores = score(*work[0])
+            s_buf[0, :, :num_keys] = score(*work[0])
             for i, (loaded, tile) in enumerate(work):
-                following = score(*work[i + 1]) if i + 1 < len(work) else None
-                absorb(loaded, tile, scores)
-                scores = following
+                if i + 1 < len(work):
+                    s_buf[(i + 1) % 2, :, :num_keys] = score(*work[i + 1])
+                absorb(loaded, tile, i % 2)
             if is_last:
                 output(step).start()
             return carry
@@ -334,9 +337,12 @@
             pltpu.VMEM((3, NUM_X, 2, 16, TOK), jnp.int32),
             pltpu.VMEM((TOK, KVH * GROUPS * HD), jnp.bfloat16),
             pltpu.VMEM((TOK, KVH * GROUPS * HD), jnp.bfloat16),
-            pltpu.VMEM((KVH, ACC_ROWS, ROWS), jnp.float32),
-            pltpu.VMEM((KVH, 8, ROWS), jnp.float32),
+            pltpu.VMEM((KVH, ROWS, 2 * HD), jnp.float32),
+            pltpu.VMEM((KVH, ROWS, HD), jnp.float32),
             pltpu.VMEM((MAX_KEYS, HD), jnp.bfloat16),
+            pltpu.VMEM((2, TILE, MAX_KEYS), jnp.float32),
+            pltpu.VMEM((2, TILE, MAX_KEYS), jnp.bfloat16),
+            pltpu.VMEM((2, TILE, HD), jnp.float32),
             dma((3, 2)),
             dma((NUM_OUT,)),
             dma((3, NUM_X, 3)),

time: 91.6 us -> 90.2 us (0.985)
  Pallas kernels: 91.3 us -> 89.9 us
    pallas_call x1, Pallas kernels: 88.9 us -> 87.5 us  [body(): pl.pallas_call(kernel, out_shape=out_shape, in_specs=[any_spec, any_spec,...]
where the time goes in v6:
time: 90.2 us; the launch traced here: 90.1 us
  Pallas kernels  89.9 us (100%)
    pallas_call x1, Pallas kernels, body(): pl.pallas_call(kernel, out_shape=out_shape, in_specs=[any_spec, any_spec,...  87.5 us
    pallas_call x1, Pallas kernels, body(): pl.pallas_call(copy_kernel, out_shape=out_shape, in_specs=[any_spec], out...  2.4 us

profile of v6, /device:TPU:1, one launch (start us, length us, event | category | flops | bytes accessed | tf_op | source)
XLA Modules:
  0.0 90.1 jit_solution(15638297199287443196)
XLA Ops:
  0.0 87.5 %shard_map.55.source = bf16[1,128,8192]{2,1,0:T(8,128)(2,1)} custom-call(bf16[1,128,8192]{2,1,0:T(8,128)(2,1)} %q_hbm.1, bf16[1,128,1024]{2,1,0:T(8,128)(2,1)} %k_hbm.1, bf16[1,128,1024]{2,1,0:T(8,128)(2,1)} %v_hbm.1, s32[1,2]{1,0:T(1,128)} %place_ref.1, s32[32]{0:T(128)} %len_ref.1), custom_call_target="tpu_custom_call" | custom-call | flops 12884901888 | bytes 5242880 | tf_op jit(solution)/shard_map/pallas_call | solution.py:330
  87.5 2.4 %shard_map.56 = bf16[1,128,8192]{2,1,0:T(8,128)(2,1)} custom-call(bf16[1,128,8192]{2,1,0:T(8,128)(2,1)} %shard_map.55.source), custom_call_target="tpu_custom_call" | custom-call | tf_op jit(solution)/shard_map/pallas_call | solution.py:360

commit v7 on v4

v7 whole, which is shorter than its diff:
```python
import math

import jax
import jax.numpy as jnp
from jax import lax
from jax.experimental import pallas as pl
from jax.experimental.pallas import tpu as pltpu
from jax.sharding import PartitionSpec as P

HD = 128
KVH = 8
GROUPS = 8
STRETCH = 64
TOK = 128
COL_STRETCHES = 16
REQS = 32
NUM_X = 4
NUM_GRP = 32
ROWS = GROUPS * TOK
TILE = 512
CORE_HEADS = KVH // 2
HALF_HEADS = CORE_HEADS // 2
HALF_LANES = HALF_HEADS * HD
CORE_LANES = CORE_HEADS * HD
HALF_OUT = HALF_HEADS * GROUPS * HD
CORE_OUT = CORE_HEADS * GROUPS * HD
CHIP_TOK = 2 * TOK
MAX_KEYS = 512
COPY_PARTS = TOK // 16

HIDDEN = -2e30
SCALE = math.log2(math.e) / math.sqrt(HD)
MESH = pl.DeviceIdType.MESH
H0, H1, POS = 0, 1, 2


def kernel(q_hbm, k_hbm, v_hbm, place_ref, len_ref, out_hbm,
           kvbuf, pbuf, q_vm, out_vm, acc, run_max, extra, which,
           local_sem, swap_send, swap_recv, out_sem, recv_ici, send_z, send_x):
    ctx = lax.axis_index("ctx")
    grp = lax.axis_index("grp")
    x = ctx // 2
    core = ctx % 2
    right = (((x + 1) % NUM_X) * 2 + core, grp)
    left = (((x + NUM_X - 1) % NUM_X) * 2 + core, grp)
    sibling = (x * 2 + 1 - core, grp)
    after = (ctx, (grp + 1) % NUM_GRP)
    before = (ctx, (grp + NUM_GRP - 1) % NUM_GRP)

    def lanes_of(which_core, half, core_lanes, half_lanes):
        start = which_core * core_lanes + half * half_lanes
        return pl.ds(pl.multiple_of(start, half_lanes), half_lanes)

    local = []
    for half in range(2):
        for part, source in enumerate((k_hbm, v_hbm)):
            local.append(pltpu.make_async_copy(
                source.at[0, :, lanes_of(core, half, CORE_LANES, HALF_LANES)],
                kvbuf.at[0, 0, half, part, 0:TOK], local_sem.at[half, part]))
    queries_in = []
    for half in range(2):
        queries_in.append(pltpu.make_async_copy(
            q_hbm.at[0, :, lanes_of(core, half, CORE_OUT, HALF_OUT)],
            q_vm.at[0, :, half * HALF_OUT:(half + 1) * HALF_OUT], local_sem.at[2, half]))
    for copy in local + queries_in:
        copy.start()

    for slot in range(2):
        pbuf[0, 0, 8 * slot:8 * slot + 8] = jnp.full(
            (8, TOK), grp * COL_STRETCHES + place_ref[0, slot], jnp.int32)

    barrier = pltpu.get_barrier_semaphore()
    for device in (right, left, sibling, after, before):
        pl.semaphore_signal(barrier, inc=1, device_id=device, device_id_type=MESH)
    pl.semaphore_wait(barrier, 5)

    started = []

    def remote(src, dst, send_sem, recv_sem, device):
        return pltpu.make_async_remote_copy(
            src_ref=src, dst_ref=dst, send_sem=send_sem, recv_sem=recv_sem,
            device_id=device, device_id_type=MESH)

    swaps = [remote(pbuf.at[0, 0, 0:16], pbuf.at[0, 0, 16:32], swap_send.at[0], swap_recv.at[0], sibling)]
    for half in range(2):
        for part, source in enumerate((k_hbm, v_hbm)):
            i = 1 + 2 * half + part
            swaps.append(remote(
                source.at[0, :, lanes_of(1 - core, half, CORE_LANES, HALF_LANES)],
                kvbuf.at[0, 0, half, part, TOK:CHIP_TOK], swap_send.at[i], swap_recv.at[i], sibling))
    for half in range(2):
        swaps.append(remote(
            q_hbm.at[0, :, lanes_of(1 - core, half, CORE_OUT, HALF_OUT)],
            q_vm.at[1, :, half * HALF_OUT:(half + 1) * HALF_OUT],
            swap_send.at[5 + half], swap_recv.at[5 + half], sibling))
    for swap in swaps[:5]:
        swap.start()

    def unit(kind, d, rx):
        if kind == POS:
            return pbuf.at[d, rx]
        return kvbuf.at[d, rx, kind]

    def send(kind, src, dst, sem, device):
        copy = remote(unit(kind, *src), unit(kind, *dst), sem, recv_ici.at[dst[0], dst[1], kind], device)
        copy.start()
        started.append(copy)

    def to_after(d, rx, kind):
        send(kind, (d, rx), (d + 1, rx), send_z.at[d, rx, kind], after)

    def to_right(d, rx, kind):
        send(kind, (d, rx), (d, 1 if rx == 0 else 3), send_x.at[d, 0, rx, kind], right)

    def to_left(d, rx, kind):
        send(kind, (d, rx), (d, 2 if rx == 0 else 3), send_x.at[d, 1, rx, kind], left)

    waited = set()

    def got(d, rx, kind):
        if (d, rx, kind) in waited:
            return
        waited.add((d, rx, kind))
        if (d, rx) != (0, 0):
            ref = unit(kind, d, rx)
            remote(ref, ref, local_sem.at[3, 0], recv_ici.at[d, rx, kind], sibling).wait_recv()
        if rx == 0:
            if kind == POS:
                to_right(d, 0, POS)
                to_left(d, 0, POS)
            elif kind == H0:
                to_right(d, 0, H0)
            else:
                to_left(d, 0, H1)
            if d < 2:
                to_after(d, 0, kind)
            if kind == H1:
                to_right(d, 0, H1)
                to_left(d, 0, H0)
        elif rx == 1 and d != 1 and kind in (POS, H0):
            to_right(d, 1, kind)
        elif rx == 2 and d != 1 and kind == H1:
            to_left(d, 2, kind)
        elif rx == 3 and d == 0:
            to_after(d, 3, kind)

    swaps[0].wait_recv()
    got(0, 0, POS)
    for half in range(2):
        for part in range(2):
            local[2 * half + part].wait()
            swaps[1 + 2 * half + part].wait_recv()
        got(0, 0, half)
    for swap in swaps[5:]:
        swap.start()

    lane = lax.broadcasted_iota(jnp.int32, (8, TOK), 1)
    highs = jnp.full((8, TOK), -1, jnp.int32)
    for t in range(4):
        highs = jnp.where(lane == t, pbuf[0, 0, 8 * t:8 * t + 8, :], highs)
    lows = jnp.zeros((8, TOK), jnp.int32)
    end = jnp.int32(0)
    for r in range(REQS):
        end = end + len_ref[r]
        lows = jnp.where(end <= highs, end, lows)

    token = lax.broadcasted_iota(jnp.int32, (TILE, HD), 0) % TOK
    column = lax.broadcasted_iota(jnp.int32, (TILE, HD), 1)
    for side in range(2):
        which[side] = jnp.where(token // STRETCH + 2 * side == column, 1.0, 0.0).astype(jnp.bfloat16)

    def causal():
        row = lax.broadcasted_iota(jnp.int32, (TOK, TOK), 0)
        col = lax.broadcasted_iota(jnp.int32, (TOK, TOK), 1)
        later = (row // STRETCH == col // STRETCH) & (col > row)
        return jnp.where(later, HIDDEN, 0.0)

    def attend(chunks, halves=(H0, H1), sides=(0, 1), is_first=False, is_last=False):
        for d, rx in chunks:
            for kind in (POS,) + halves:
                got(d, rx, kind)
        num_keys = CHIP_TOK * len(chunks)
        for i, (d, rx) in enumerate(chunks):
            for t in range(4):
                stretch = pbuf[d, rx, 8 * t:8 * t + 8, :]
                hide = jnp.where((stretch >= lows) & (stretch <= highs), 0.0, HIDDEN)
                at = i * CHIP_TOK + t * STRETCH
                extra[at:at + STRETCH, :] = jnp.concatenate([hide] * 8, axis=0).astype(jnp.bfloat16)

        def load(half, inner):
            lanes = slice(inner * HD, (inner + 1) * HD)
            keys = jnp.concatenate([kvbuf[d, rx, half, 0, :, lanes] for d, rx in chunks], axis=0)
            vals = jnp.concatenate([kvbuf[d, rx, half, 1, :, lanes] for d, rx in chunks], axis=0)
            keys = jnp.concatenate([keys, extra[:num_keys, :]], axis=1)
            vals = jnp.concatenate([vals, jnp.ones_like(vals)], axis=1)
            return half * HALF_HEADS + inner, keys, vals

        def score(loaded, side, tile):
            head, keys, _ = loaded
            queries = []
            for j in range(TILE // TOK):
                group = tile * (TILE // TOK) + j
                lanes = pl.ds(pl.multiple_of((head * GROUPS + group) * HD, HD), HD)
                queries.append(q_vm[side, :, lanes])
            queries = jnp.concatenate([jnp.concatenate(queries, axis=0), which[side]], axis=1)
            return lax.dot_general(
                queries, keys, (((1,), (1,)), ((), ())), preferred_element_type=jnp.float32)

        def absorb(loaded, side, tile, scores):
            head, _, vals = loaded
            rows = slice(tile * TILE, (tile + 1) * TILE)
            if is_first:
                own = scores[:, side * TOK:(side + 1) * TOK]
                own = (own.reshape(TILE // TOK, TOK, TOK) + causal()[None]).reshape(TILE, TOK)
                both = (own, scores[:, TOK:]) if side == 0 else (scores[:, :TOK], own)
                scores = jnp.concatenate(both, axis=1)
            top = jnp.broadcast_to(jnp.max(scores, axis=1, keepdims=True), (TILE, HD)) * SCALE
            if not is_first:
                old = run_max[head, side, rows]
                top = jnp.maximum(old, top)
            tops = jnp.concatenate([top] * (num_keys // HD), axis=1)
            weights = jnp.exp2(scores * SCALE - tops).astype(jnp.bfloat16)
            part = lax.dot_general(
                weights, vals, (((1,), (0,)), ((), ())),
                preferred_element_type=jnp.float32)
            if not is_first:
                factor = jnp.exp2(old - top)
                part = part + acc[head, side, rows] * jnp.concatenate([factor, factor], axis=1)
            if is_last:
                result = (part[:, :HD] / part[:, HD:]).astype(jnp.bfloat16)
                for j in range(TILE // TOK):
                    group = tile * (TILE // TOK) + j
                    place = pl.ds(pl.multiple_of((head * GROUPS + group) * HD, HD), HD)
                    out_vm[side, :, place] = result[j * TOK:(j + 1) * TOK]
            else:
                acc[head, side, rows] = part
                run_max[head, side, rows] = top

        def some_heads(step, carry):
            half = halves[0] if len(halves) == 1 else step % 2
            side = sides[0] if len(sides) == 1 else step // len(halves)
            work = []
            for i in range(HALF_HEADS):
                loaded = load(half, i)
                work += [(loaded, side, tile) for tile in range(ROWS // TILE)]
            scores = score(*work[0])
            for i, item in enumerate(work):
                following = score(*work[i + 1]) if i + 1 < len(work) else None
                absorb(*item, scores)
                scores = following
            if is_last:
                output(half, side).start()
            return carry

        lax.fori_loop(0, len(halves) * len(sides), some_heads, 0)

    def output(half, side):
        source = out_vm.at[side, :, pl.ds(pl.multiple_of(half * HALF_OUT, HALF_OUT), HALF_OUT)]
        target = out_hbm.at[0, :, lanes_of(core, half, CORE_OUT, HALF_OUT)]
        if side == 0:
            return pltpu.make_async_copy(source, target, out_sem.at[0, half])
        return remote(source, target, out_sem.at[1, half], out_sem.at[2, half], sibling)

    for copy in queries_in:
        copy.wait()
    attend([(0, 0)], sides=(0,), is_first=True)
    for swap in swaps[5:]:
        swap.wait_recv()
    attend([(0, 0)], sides=(1,), is_first=True)

    got(0, 1, POS)
    got(0, 1, H0)
    got(0, 2, H1)
    got(1, 0, POS)
    got(1, 0, H0)
    attend([(0, 1)], (H0,))
    attend([(0, 2)], (H1,))
    got(1, 0, H1)
    attend([(0, 1), (1, 0)], (H1,))
    attend([(0, 2), (1, 0)], (H0,))
    for kind in (POS, H0, H1):
        got(0, 3, kind)
    got(2, 0, POS)
    got(2, 0, H0)
    attend([(0, 3)])
    got(2, 0, H1)
    attend([(2, 0), (1, 1)], (H0,))
    attend([(2, 0), (1, 2)], (H1,))
    got(1, 1, H1)
    got(1, 2, H0)
    attend([(1, 1), (1, 3)], (H1,))
    got(2, 1, POS)
    got(2, 1, H0)
    got(2, 2, H1)
    attend([(1, 2), (1, 3)], (H0,))
    attend([(2, 1), (2, 2)])
    attend([(2, 3)], sides=(1,), is_last=True)
    attend([(2, 3)], sides=(0,), is_last=True)

    for half in range(2):
        output(half, 0).wait()
        output(half, 1).wait()
    for copy in swaps + started:
        copy.wait_send()


def copy_kernel(source, target, held, sems):
    parts = []
    for part in range(COPY_PARTS):
        rows = slice(part * 16, (part + 1) * 16)
        parts.append((
            pltpu.make_async_copy(source.at[0, rows], held.at[rows], sems.at[0, part]),
            pltpu.make_async_copy(held.at[rows], target.at[0, rows], sems.at[1, part])))
    for come, _ in parts:
        come.start()
    for come, leave in parts:
        come.wait()
        leave.start()
    for _, leave in parts:
        leave.wait()


def body(queries, keys, values, placement, lengths):
    any_spec = pl.BlockSpec(memory_space=pl.ANY)
    smem = pl.BlockSpec(memory_space=pltpu.SMEM)
    dma = pltpu.SemaphoreType.DMA
    out_shape = jax.ShapeDtypeStruct((1, TOK, KVH * GROUPS * HD), jnp.bfloat16)
    result = pl.pallas_call(
        kernel,
        out_shape=out_shape,
        in_specs=[any_spec, any_spec, any_spec, smem, smem],
        out_specs=any_spec,
        scratch_shapes=[
            pltpu.VMEM((3, NUM_X, 2, 2, CHIP_TOK, HALF_LANES), jnp.bfloat16),
            pltpu.VMEM((3, NUM_X, 32, TOK), jnp.int32),
            pltpu.VMEM((2, TOK, CORE_OUT), jnp.bfloat16),
            pltpu.VMEM((2, TOK, CORE_OUT), jnp.bfloat16),
            pltpu.VMEM((CORE_HEADS, 2, ROWS, 2 * HD), jnp.float32),
            pltpu.VMEM((CORE_HEADS, 2, ROWS, HD), jnp.float32),
            pltpu.VMEM((MAX_KEYS, HD), jnp.bfloat16),
            pltpu.VMEM((2, TILE, HD), jnp.bfloat16),
            dma((4, 2)),
            dma((7,)),
            dma((7,)),
            dma((3, 2)),
            dma((3, NUM_X, 3)),
            dma((2, NUM_X, 3)),
            dma((3, 2, 3, 3)),
        ],
        compiler_params=pltpu.CompilerParams(
            collective_id=0, has_side_effects=True, vmem_limit_bytes=56 * 1024 * 1024),
        cost_estimate=pl.CostEstimate(
            flops=4 * TOK * 64 * 3072 * HD, bytes_accessed=5 * 1024 * 1024,
            transcendentals=TOK * 64 * 3072),
    )(queries, keys, values, placement, lengths)
    return pl.pallas_call(
        copy_kernel,
        out_shape=out_shape,
        in_specs=[any_spec],
        out_specs=any_spec,
        scratch_shapes=[
            pltpu.VMEM((TOK, KVH * GROUPS * HD), jnp.bfloat16),
            dma((2, COPY_PARTS)),
        ],
        compiler_params=pltpu.CompilerParams(vmem_limit_bytes=56 * 1024 * 1024),
    )(result)


def solution(mesh):
    in_specs = (
        P("grp", "ctx", None),
        P("grp", "ctx", None),
        P("grp", "ctx", None),
        P("grp", "ctx"),
        P(),
    )
    out_specs = P("grp", "ctx", None)
    return jax.shard_map(body, mesh=mesh, in_specs=in_specs, out_specs=out_specs, check_vma=False)
```

time: 91.6 us -> 71.7 us (0.78)
  Pallas kernels: 91.3 us -> 71.4 us
    pallas_call x1, Pallas kernels: 88.9 us -> 69 us  [body(): pl.pallas_call(kernel, out_shape=out_shape, in_specs=[any_spec, any_spec,...]
where the time goes in v7:
time: 71.7 us; the launch traced here: 71.6 us
  Pallas kernels  71.4 us (100%)
    pallas_call x1, Pallas kernels, body(): pl.pallas_call(kernel, out_shape=out_shape, in_specs=[any_spec, any_spec,...  69 us
    pallas_call x1, Pallas kernels, body(): pl.pallas_call(copy_kernel, out_shape=out_shape, in_specs=[any_spec], out...  2.4 us

profile of v7, /device:TPU:1, one launch (start us, length us, event | category | flops | bytes accessed | tf_op | source)
XLA Modules:
  0.0 71.6 jit_solution(3939063077781071827)
XLA Ops:
  0.0 69.0 %shard_map.55.source = bf16[1,128,8192]{2,1,0:T(8,128)(2,1)} custom-call(bf16[1,128,8192]{2,1,0:T(8,128)(2,1)} %q_hbm.1, bf16[1,128,1024]{2,1,0:T(8,128)(2,1)} %k_hbm.1, bf16[1,128,1024]{2,1,0:T(8,128)(2,1)} %v_hbm.1, s32[1,2]{1,0:T(1,128)} %place_ref.1, s32[32]{0:T(128)} %len_ref.1), custom_call_target="tpu_custom_call" | custom-call | flops 12884901888 | bytes 5242880 | tf_op jit(solution)/shard_map/pallas_call | solution.py:328
  69.0 2.4 %shard_map.56 = bf16[1,128,8192]{2,1,0:T(8,128)(2,1)} custom-call(bf16[1,128,8192]{2,1,0:T(8,128)(2,1)} %shard_map.55.source), custom_call_target="tpu_custom_call" | custom-call | tf_op jit(solution)/shard_map/pallas_call | solution.py:356

commit v8 on v7

--- a/solution.py
+++ b/solution.py
@@ -22,21 +22,22 @@
 HALF_HEADS = CORE_HEADS // 2
 HALF_LANES = HALF_HEADS * HD
 CORE_LANES = CORE_HEADS * HD
-HALF_OUT = HALF_HEADS * GROUPS * HD
+HEAD_OUT = GROUPS * HD
+HALF_OUT = HALF_HEADS * HEAD_OUT
 CORE_OUT = CORE_HEADS * GROUPS * HD
 CHIP_TOK = 2 * TOK
-MAX_KEYS = 512
+MAX_KEYS = 768
 COPY_PARTS = TOK // 16
 
 HIDDEN = -2e30
 SCALE = math.log2(math.e) / math.sqrt(HD)
 MESH = pl.DeviceIdType.MESH
-H0, H1, POS = 0, 1, 2
+H0, H1, POS, K1, V1 = 0, 1, 2, 3, 4
 
 
 def kernel(q_hbm, k_hbm, v_hbm, place_ref, len_ref, out_hbm,
            kvbuf, pbuf, q_vm, out_vm, acc, run_max, extra, which,
-           local_sem, swap_send, swap_recv, out_sem, recv_ici, send_z, send_x):
+           local_sem, swap_send, swap_recv, out_sem, recv_ici, send_z, send_x, send_own):
     ctx = lax.axis_index("ctx")
     grp = lax.axis_index("grp")
     x = ctx // 2
@@ -99,6 +100,8 @@
     def unit(kind, d, rx):
         if kind == POS:
             return pbuf.at[d, rx]
+        if kind in (K1, V1):
+            return kvbuf.at[d, rx, H1, kind - K1]
         return kvbuf.at[d, rx, kind]
 
     def send(kind, src, dst, sem, device):
@@ -115,44 +118,91 @@
     def to_left(d, rx, kind):
         send(kind, (d, rx), (d, 2 if rx == 0 else 3), send_x.at[d, 1, rx, kind], left)
 
+    def own_tokens(i, half, dst, device):
+        for part, source in enumerate((k_hbm, v_hbm)):
+            copy = remote(
+                source.at[0, :, lanes_of(core, half, CORE_LANES, HALF_LANES)],
+                kvbuf.at[dst[0], dst[1], half, part, 0:TOK],
+                send_own.at[i, part], recv_ici.at[dst[0], dst[1], half], device)
+            copy.start()
+            started.append(copy)
+
+    def swapped_tokens(i, half, dst, device):
+        copy = remote(
+            kvbuf.at[0, 0, half, :, TOK:CHIP_TOK], kvbuf.at[dst[0], dst[1], half, :, TOK:CHIP_TOK],
+            send_own.at[i, 2], recv_ici.at[dst[0], dst[1], half], device)
+        copy.start()
+        started.append(copy)
+
+    own_sends = (
+        (H0, (0, 1), right), (H0, (1, 0), after), (H1, (0, 2), left),
+        (H1, (1, 0), after), (H1, (0, 1), right), (H0, (0, 2), left))
+    for i in range(3):
+        own_tokens(i, *own_sends[i])
+    swaps[0].wait_recv()
+    to_right(0, 0, POS)
+    to_left(0, 0, POS)
+    to_after(0, 0, POS)
+    for part in range(2):
+        swaps[1 + part].wait_recv()
+    swapped_tokens(0, *own_sends[0])
+    swapped_tokens(1, *own_sends[1])
+    for part in range(2):
+        swaps[3 + part].wait_recv()
+    swapped_tokens(2, *own_sends[2])
+    for i in range(3, 6):
+        own_tokens(i, *own_sends[i])
+        swapped_tokens(i, *own_sends[i])
+    for swap in swaps[5:]:
+        swap.start()
+    for copy in local:
+        copy.wait()
+
     waited = set()
+    for kind in (POS, H0, H1):
+        waited.add((0, 0, kind))
 
     def got(d, rx, kind):
         if (d, rx, kind) in waited:
             return
         waited.add((d, rx, kind))
-        if (d, rx) != (0, 0):
-            ref = unit(kind, d, rx)
-            remote(ref, ref, local_sem.at[3, 0], recv_ici.at[d, rx, kind], sibling).wait_recv()
-        if rx == 0:
+        ref = unit(kind, d, rx)
+        remote(ref, ref, local_sem.at[3, 0], recv_ici.at[d, rx, kind], sibling).wait_recv()
+        if d == 1 and rx == 0:
             if kind == POS:
-                to_right(d, 0, POS)
-                to_left(d, 0, POS)
+                to_right(1, 0, POS)
+                to_left(1, 0, POS)
+                to_after(1, 0, POS)
             elif kind == H0:
-                to_right(d, 0, H0)
+                to_right(1, 0, H0)
+                to_after(1, 0, H0)
             else:
-                to_left(d, 0, H1)
-            if d < 2:
-                to_after(d, 0, kind)
-            if kind == H1:
-                to_right(d, 0, H1)
-                to_left(d, 0, H0)
-        elif rx == 1 and d != 1 and kind in (POS, H0):
-            to_right(d, 1, kind)
-        elif rx == 2 and d != 1 and kind == H1:
-            to_left(d, 2, kind)
-        elif rx == 3 and d == 0:
-            to_after(d, 3, kind)
-
-    swaps[0].wait_recv()
-    got(0, 0, POS)
-    for half in range(2):
-        for part in range(2):
-            local[2 * half + part].wait()
-            swaps[1 + 2 * half + part].wait_recv()
-        got(0, 0, half)
-    for swap in swaps[5:]:
-        swap.start()
+                to_left(1, 0, H1)
+                to_after(1, 0, H1)
+                to_right(1, 0, H1)
+                to_left(1, 0, H0)
+        elif d == 2 and rx == 0:
+            if kind == POS:
+                to_right(2, 0, POS)
+                to_left(2, 0, POS)
+            elif kind == H1:
+                got(2, 0, H0)
+                to_right(2, 0, H1)
+                to_left(2, 0, H1)
+                to_right(2, 0, H0)
+                to_left(2, 0, H0)
+        elif d == 0 and rx == 1 and kind in (POS, H0):
+            to_right(0, 1, kind)
+        elif d == 0 and rx == 2 and kind == H1:
+            to_left(0, 2, H1)
+        elif d == 0 and rx == 3:
+            to_after(0, 3, kind)
+        elif d == 1 and rx == 3 and kind in (POS, H0):
+            to_after(1, 3, kind)
+        elif d == 2 and rx == 1 and kind == H1:
+            to_right(2, 1, K1)
+        elif d == 2 and rx == 2 and kind == H1:
+            to_left(2, 2, V1)
 
     lane = lax.broadcasted_iota(jnp.int32, (8, TOK), 1)
     highs = jnp.full((8, TOK), -1, jnp.int32)
@@ -178,7 +228,11 @@
     def attend(chunks, halves=(H0, H1), sides=(0, 1), is_first=False, is_last=False):
         for d, rx in chunks:
             for kind in (POS,) + halves:
-                got(d, rx, kind)
+                if (d, rx, kind) == (2, 3, H1):
+                    got(2, 3, K1)
+                    got(2, 3, V1)
+                else:
+                    got(d, rx, kind)
         num_keys = CHIP_TOK * len(chunks)
         for i, (d, rx) in enumerate(chunks):
             for t in range(4):
@@ -248,18 +302,18 @@
                 following = score(*work[i + 1]) if i + 1 < len(work) else None
                 absorb(*item, scores)
                 scores = following
-            if is_last:
-                output(half, side).start()
+                if is_last and item[2] == ROWS // TILE - 1:
+                    output(item[0][0], side).start()
             return carry
 
         lax.fori_loop(0, len(halves) * len(sides), some_heads, 0)
 
-    def output(half, side):
-        source = out_vm.at[side, :, pl.ds(pl.multiple_of(half * HALF_OUT, HALF_OUT), HALF_OUT)]
-        target = out_hbm.at[0, :, lanes_of(core, half, CORE_OUT, HALF_OUT)]
+    def output(head, side):
+        source = out_vm.at[side, :, pl.ds(head * HEAD_OUT, HEAD_OUT)]
+        target = out_hbm.at[0, :, lanes_of(core, head, CORE_OUT, HEAD_OUT)]
         if side == 0:
-            return pltpu.make_async_copy(source, target, out_sem.at[0, half])
-        return remote(source, target, out_sem.at[1, half], out_sem.at[2, half], sibling)
+            return pltpu.make_async_copy(source, target, out_sem.at[0, head])
+        return remote(source, target, out_sem.at[1, head], out_sem.at[2, head], sibling)
 
     for copy in queries_in:
         copy.wait()
@@ -286,20 +340,21 @@
     got(2, 0, H1)
     attend([(2, 0), (1, 1)], (H0,))
     attend([(2, 0), (1, 2)], (H1,))
-    got(1, 1, H1)
-    got(1, 2, H0)
+    attend([(1, 2), (1, 3)], (H0,))
+    got(2, 1, POS)
+    got(2, 2, POS)
+    got(2, 1, H1)
+    got(2, 2, H1)
     attend([(1, 1), (1, 3)], (H1,))
-    got(2, 1, POS)
-    got(2, 1, H0)
-    got(2, 2, H1)
-    attend([(1, 2), (1, 3)], (H0,))
-    attend([(2, 1), (2, 2)])
-    attend([(2, 3)], sides=(1,), is_last=True)
-    attend([(2, 3)], sides=(0,), is_last=True)
-
-    for half in range(2):
-        output(half, 0).wait()
-        output(half, 1).wait()
+    attend([(2, 1), (2, 2)], (H1,))
+    for side in (1, 0):
+        attend([(2, 1), (2, 2), (2, 3)], (H0,), sides=(side,), is_last=True)
+    for side in (1, 0):
+        attend([(2, 3)], (H1,), sides=(side,), is_last=True)
+
+    for head in range(CORE_HEADS):
+        output(head, 0).wait()
+        output(head, 1).wait()
     for copy in swaps + started:
         copy.wait_send()
 
@@ -342,10 +397,11 @@
             dma((4, 2)),
             dma((7,)),
             dma((7,)),
-            dma((3, 2)),
-            dma((3, NUM_X, 3)),
+            dma((3, CORE_HEADS)),
+            dma((3, NUM_X, 5)),
             dma((2, NUM_X, 3)),
-            dma((3, 2, 3, 3)),
+            dma((3, 2, 3, 5)),
+            dma((6, 3)),
         ],
         compiler_params=pltpu.CompilerParams(
             collective_id=0, has_side_effects=True, vmem_limit_bytes=56 * 1024 * 1024),

time: 71.7 us -> 68.9 us (0.961)
  Pallas kernels: 71.4 us -> 68.6 us
    pallas_call x1, Pallas kernels: 69 us -> 66.2 us  [body(): pl.pallas_call(kernel, out_shape=out_shape, in_specs=[any_spec, any_spec,...]
where the time goes in v8:
time: 68.9 us; the launch traced here: 68.8 us
  Pallas kernels  68.6 us (100%)
    pallas_call x1, Pallas kernels, body(): pl.pallas_call(kernel, out_shape=out_shape, in_specs=[any_spec, any_spec,...  66.2 us
    pallas_call x1, Pallas kernels, body(): pl.pallas_call(copy_kernel, out_shape=out_shape, in_specs=[any_spec], out...  2.4 us

profile of v8, /device:TPU:1, one launch (start us, length us, event | category | flops | bytes accessed | tf_op | source)
XLA Modules:
  0.0 68.8 jit_solution(14175535623863451723)
XLA Ops:
  0.0 66.2 %shard_map.55.source = bf16[1,128,8192]{2,1,0:T(8,128)(2,1)} custom-call(bf16[1,128,8192]{2,1,0:T(8,128)(2,1)} %q_hbm.1, bf16[1,128,1024]{2,1,0:T(8,128)(2,1)} %k_hbm.1, bf16[1,128,1024]{2,1,0:T(8,128)(2,1)} %v_hbm.1, s32[1,2]{1,0:T(1,128)} %place_ref.1, s32[32]{0:T(128)} %len_ref.1), custom_call_target="tpu_custom_call" | custom-call | flops 12884901888 | bytes 5242880 | tf_op jit(solution)/shard_map/pallas_call | solution.py:383
  66.2 2.4 %shard_map.56 = bf16[1,128,8192]{2,1,0:T(8,128)(2,1)} custom-call(bf16[1,128,8192]{2,1,0:T(8,128)(2,1)} %shard_map.55.source), custom_call_target="tpu_custom_call" | custom-call | tf_op jit(solution)/shard_map/pallas_call | solution.py:412

commit v9 on v8

--- a/solution.py
+++ b/solution.py
@@ -32,7 +32,7 @@
 HIDDEN = -2e30
 SCALE = math.log2(math.e) / math.sqrt(HD)
 MESH = pl.DeviceIdType.MESH
-H0, H1, POS, K1, V1 = 0, 1, 2, 3, 4
+H0, H1, POS = 0, 1, 2
 
 
 def kernel(q_hbm, k_hbm, v_hbm, place_ref, len_ref, out_hbm,
@@ -47,6 +47,10 @@
     sibling = (x * 2 + 1 - core, grp)
     after = (ctx, (grp + 1) % NUM_GRP)
     before = (ctx, (grp + NUM_GRP - 1) % NUM_GRP)
+
+    barrier = pltpu.get_barrier_semaphore()
+    for device in (right, left, sibling, after, before):
+        pl.semaphore_signal(barrier, inc=1, device_id=device, device_id_type=MESH)
 
     def lanes_of(which_core, half, core_lanes, half_lanes):
         start = which_core * core_lanes + half * half_lanes
@@ -70,9 +74,6 @@
         pbuf[0, 0, 8 * slot:8 * slot + 8] = jnp.full(
             (8, TOK), grp * COL_STRETCHES + place_ref[0, slot], jnp.int32)
 
-    barrier = pltpu.get_barrier_semaphore()
-    for device in (right, left, sibling, after, before):
-        pl.semaphore_signal(barrier, inc=1, device_id=device, device_id_type=MESH)
     pl.semaphore_wait(barrier, 5)
 
     started = []
@@ -100,8 +101,6 @@
     def unit(kind, d, rx):
         if kind == POS:
             return pbuf.at[d, rx]
-        if kind in (K1, V1):
-            return kvbuf.at[d, rx, H1, kind - K1]
         return kvbuf.at[d, rx, kind]
 
     def send(kind, src, dst, sem, device):
@@ -150,11 +149,11 @@
     for part in range(2):
         swaps[3 + part].wait_recv()
     swapped_tokens(2, *own_sends[2])
+    for swap in swaps[5:]:
+        swap.start()
     for i in range(3, 6):
         own_tokens(i, *own_sends[i])
         swapped_tokens(i, *own_sends[i])
-    for swap in swaps[5:]:
-        swap.start()
     for copy in local:
         copy.wait()
 
@@ -197,12 +196,8 @@
             to_left(0, 2, H1)
         elif d == 0 and rx == 3:
             to_after(0, 3, kind)
-        elif d == 1 and rx == 3 and kind in (POS, H0):
+        elif d == 1 and rx == 3:
             to_after(1, 3, kind)
-        elif d == 2 and rx == 1 and kind == H1:
-            to_right(2, 1, K1)
-        elif d == 2 and rx == 2 and kind == H1:
-            to_left(2, 2, V1)
 
     lane = lax.broadcasted_iota(jnp.int32, (8, TOK), 1)
     highs = jnp.full((8, TOK), -1, jnp.int32)
@@ -228,11 +223,7 @@
     def attend(chunks, halves=(H0, H1), sides=(0, 1), is_first=False, is_last=False):
         for d, rx in chunks:
             for kind in (POS,) + halves:
-                if (d, rx, kind) == (2, 3, H1):
-                    got(2, 3, K1)
-                    got(2, 3, V1)
-                else:
-                    got(d, rx, kind)
+                got(d, rx, kind)
         num_keys = CHIP_TOK * len(chunks)
         for i, (d, rx) in enumerate(chunks):
             for t in range(4):
@@ -318,15 +309,14 @@
     for copy in queries_in:
         copy.wait()
     attend([(0, 0)], sides=(0,), is_first=True)
-    for swap in swaps[5:]:
-        swap.wait_recv()
-    attend([(0, 0)], sides=(1,), is_first=True)
-
     got(0, 1, POS)
     got(0, 1, H0)
     got(0, 2, H1)
     got(1, 0, POS)
     got(1, 0, H0)
+    for swap in swaps[5:]:
+        swap.wait_recv()
+    attend([(0, 0)], sides=(1,), is_first=True)
     attend([(0, 1)], (H0,))
     attend([(0, 2)], (H1,))
     got(1, 0, H1)
@@ -398,9 +388,9 @@
             dma((7,)),
             dma((7,)),
             dma((3, CORE_HEADS)),
-            dma((3, NUM_X, 5)),
+            dma((3, NUM_X, 3)),
             dma((2, NUM_X, 3)),
-            dma((3, 2, 3, 5)),
+            dma((3, 2, 3, 3)),
             dma((6, 3)),
         ],
         compiler_params=pltpu.CompilerParams(

time: 68.9 us -> 68.3 us (level)
  no operation moved by 1% of the time
where the time goes in v9:
time: 68.3 us; the launch traced here: 68.2 us
  Pallas kernels  68.1 us (100%)
    pallas_call x1, Pallas kernels, body(): pl.pallas_call(kernel, out_shape=out_shape, in_specs=[any_spec, any_spec,...  65.7 us
    pallas_call x1, Pallas kernels, body(): pl.pallas_call(copy_kernel, out_shape=out_shape, in_specs=[any_spec], out...  2.4 us

profile of v9, /device:TPU:1, one launch (start us, length us, event | category | flops | bytes accessed | tf_op | source)
XLA Modules:
  0.0 68.2 jit_solution(5227765080335663664)
XLA Ops:
  0.0 65.7 %shard_map.55.source = bf16[1,128,8192]{2,1,0:T(8,128)(2,1)} custom-call(bf16[1,128,8192]{2,1,0:T(8,128)(2,1)} %q_hbm.1, bf16[1,128,1024]{2,1,0:T(8,128)(2,1)} %k_hbm.1, bf16[1,128,1024]{2,1,0:T(8,128)(2,1)} %v_hbm.1, s32[1,2]{1,0:T(1,128)} %place_ref.1, s32[32]{0:T(128)} %len_ref.1), custom_call_target="tpu_custom_call" | custom-call | flops 12884901888 | bytes 5242880 | tf_op jit(solution)/shard_map/pallas_call | solution.py:373
  65.7 2.4 %shard_map.56 = bf16[1,128,8192]{2,1,0:T(8,128)(2,1)} custom-call(bf16[1,128,8192]{2,1,0:T(8,128)(2,1)} %shard_map.55.source), custom_call_target="tpu_custom_call" | custom-call | tf_op jit(solution)/shard_map/pallas_call | solution.py:402

commit v10 on v8

--- a/solution.py
+++ b/solution.py
@@ -48,6 +48,10 @@
     after = (ctx, (grp + 1) % NUM_GRP)
     before = (ctx, (grp + NUM_GRP - 1) % NUM_GRP)
 
+    barrier = pltpu.get_barrier_semaphore()
+    for device in (right, left, sibling, after, before):
+        pl.semaphore_signal(barrier, inc=1, device_id=device, device_id_type=MESH)
+
     def lanes_of(which_core, half, core_lanes, half_lanes):
         start = which_core * core_lanes + half * half_lanes
         return pl.ds(pl.multiple_of(start, half_lanes), half_lanes)
@@ -70,9 +74,6 @@
         pbuf[0, 0, 8 * slot:8 * slot + 8] = jnp.full(
             (8, TOK), grp * COL_STRETCHES + place_ref[0, slot], jnp.int32)
 
-    barrier = pltpu.get_barrier_semaphore()
-    for device in (right, left, sibling, after, before):
-        pl.semaphore_signal(barrier, inc=1, device_id=device, device_id_type=MESH)
     pl.semaphore_wait(barrier, 5)
 
     started = []
@@ -150,11 +151,11 @@
     for part in range(2):
         swaps[3 + part].wait_recv()
     swapped_tokens(2, *own_sends[2])
+    for swap in swaps[5:]:
+        swap.start()
     for i in range(3, 6):
         own_tokens(i, *own_sends[i])
         swapped_tokens(i, *own_sends[i])
-    for swap in swaps[5:]:
-        swap.start()
     for copy in local:
         copy.wait()
 
@@ -318,15 +319,14 @@
     for copy in queries_in:
         copy.wait()
     attend([(0, 0)], sides=(0,), is_first=True)
-    for swap in swaps[5:]:
-        swap.wait_recv()
-    attend([(0, 0)], sides=(1,), is_first=True)
-
     got(0, 1, POS)
     got(0, 1, H0)
     got(0, 2, H1)
     got(1, 0, POS)
     got(1, 0, H0)
+    for swap in swaps[5:]:
+        swap.wait_recv()
+    attend([(0, 0)], sides=(1,), is_first=True)
     attend([(0, 1)], (H0,))
     attend([(0, 2)], (H1,))
     got(1, 0, H1)

time: 68.9 us -> 68.9 us (level)
  no operation moved by 1% of the time
where the time goes in v10:
time: 68.9 us; the launch traced here: 68.8 us
  Pallas kernels  68.6 us (100%)
    pallas_call x1, Pallas kernels, body(): pl.pallas_call(kernel, out_shape=out_shape, in_specs=[any_spec, any_spec,...  66.2 us
    pallas_call x1, Pallas kernels, body(): pl.pallas_call(copy_kernel, out_shape=out_shape, in_specs=[any_spec], out...  2.4 us

profile of v10, /device:TPU:1, one launch (start us, length us, event | category | flops | bytes accessed | tf_op | source)
XLA Modules:
  0.0 68.8 jit_solution(4359054483337974396)
XLA Ops:
  0.0 66.2 %shard_map.55.source = bf16[1,128,8192]{2,1,0:T(8,128)(2,1)} custom-call(bf16[1,128,8192]{2,1,0:T(8,128)(2,1)} %q_hbm.1, bf16[1,128,1024]{2,1,0:T(8,128)(2,1)} %k_hbm.1, bf16[1,128,1024]{2,1,0:T(8,128)(2,1)} %v_hbm.1, s32[1,2]{1,0:T(1,128)} %place_ref.1, s32[32]{0:T(128)} %len_ref.1), custom_call_target="tpu_custom_call" | custom-call | flops 12884901888 | bytes 5242880 | tf_op jit(solution)/shard_map/pallas_call | solution.py:383
  66.2 2.4 %shard_map.56 = bf16[1,128,8192]{2,1,0:T(8,128)(2,1)} custom-call(bf16[1,128,8192]{2,1,0:T(8,128)(2,1)} %shard_map.55.source), custom_call_target="tpu_custom_call" | custom-call | tf_op jit(solution)/shard_map/pallas_call | solution.py:412

commit v11 on v10

--- a/solution.py
+++ b/solution.py
@@ -327,19 +327,15 @@
     for swap in swaps[5:]:
         swap.wait_recv()
     attend([(0, 0)], sides=(1,), is_first=True)
-    attend([(0, 1)], (H0,))
-    attend([(0, 2)], (H1,))
     got(1, 0, H1)
-    attend([(0, 1), (1, 0)], (H1,))
-    attend([(0, 2), (1, 0)], (H0,))
+    attend([(0, 1), (0, 2), (1, 0)], (H1,))
+    attend([(0, 1), (0, 2), (1, 0)], (H0,))
     for kind in (POS, H0, H1):
         got(0, 3, kind)
-    got(2, 0, POS)
-    got(2, 0, H0)
-    attend([(0, 3)])
-    got(2, 0, H1)
-    attend([(2, 0), (1, 1)], (H0,))
-    attend([(2, 0), (1, 2)], (H1,))
+    for kind in (POS, H0, H1):
+        got(2, 0, kind)
+    attend([(0, 3), (2, 0), (1, 1)], (H0,))
+    attend([(0, 3), (2, 0), (1, 2)], (H1,))
     attend([(1, 2), (1, 3)], (H0,))
     got(2, 1, POS)
     got(2, 2, POS)

time: 68.9 us -> 69.1 us (level)
  no operation moved by 1% of the time
where the time goes in v11:
time: 69.1 us; the launch traced here: 69 us
  Pallas kernels  68.9 us (100%)
    pallas_call x1, Pallas kernels, body(): pl.pallas_call(kernel, out_shape=out_shape, in_specs=[any_spec, any_spec,...  66.5 us
    pallas_call x1, Pallas kernels, body(): pl.pallas_call(copy_kernel, out_shape=out_shape, in_specs=[any_spec], out...  2.4 us

profile of v11, /device:TPU:1, one launch (start us, length us, event | category | flops | bytes accessed | tf_op | source)
XLA Modules:
  0.0 69.0 jit_solution(919677154770966265)
XLA Ops:
  0.0 66.5 %shard_map.55.source = bf16[1,128,8192]{2,1,0:T(8,128)(2,1)} custom-call(bf16[1,128,8192]{2,1,0:T(8,128)(2,1)} %q_hbm.1, bf16[1,128,1024]{2,1,0:T(8,128)(2,1)} %k_hbm.1, bf16[1,128,1024]{2,1,0:T(8,128)(2,1)} %v_hbm.1, s32[1,2]{1,0:T(1,128)} %place_ref.1, s32[32]{0:T(128)} %len_ref.1), custom_call_target="tpu_custom_call" | custom-call | flops 12884901888 | bytes 5242880 | tf_op jit(solution)/shard_map/pallas_call | solution.py:379
  66.5 2.4 %shard_map.56 = bf16[1,128,8192]{2,1,0:T(8,128)(2,1)} custom-call(bf16[1,128,8192]{2,1,0:T(8,128)(2,1)} %shard_map.55.source), custom_call_target="tpu_custom_call" | custom-call | tf_op jit(solution)/shard_map/pallas_call | solution.py:408
